TPU v7x, 32 devices: a whole 2x2x4 slice. The times are simulated.
32 devices in a mesh: chan: 8 (over y, x, core), seg: 4 (over z).
Axes of the slice: x: 2, y: 2, z: 4, core: 2. Of those that a mesh axis runs over, the one named last changes fastest.
Arguments:
- traces: bfloat16 [1024, 8, 8192], P('chan', 'seg'), may hold values from -20 to 20
- pair_offsets: int32 [8, 7], replicated, may hold values from 1 to 7, as said below
- pair_counts: int32 [8], replicated, may hold values from 1 to 7, 16 in all
- pair_owner: int32 [16], replicated, may hold values from 0 to 15, each once
Outputs:
- correlations: float32 [128, 16, 128, 256], P('seg', 'chan')
Inputs may be any that keep to these rules, and one draw needn't show every extreme that they name: `pair_offsets`: row a lists 7 distinct offsets; only its first pair_counts[a] entries name pairs. `pair_counts`: the counts sum to 16. `pair_owner`: every slot number appears once.
All inputs are finite; a program needn't handle non-finite values.
Results may differ from a plain program's by a relative error of at most 0.017.
Values may be sent and summed in bfloat16 or wider, within the bound.
A program may use at most 128 MiB of HBM per device.

v0:
```python
import math

import jax
import jax.numpy as jnp
from jax import lax
from jax.sharding import PartitionSpec as P

SAMPLES = 8192
BAND_START = 32
FREQS = 512
HALF = 8
LAGS = 256
TILE_DEV = 2


def smoother(bin_count):
    bins_axis = lax.iota(jnp.int32, bin_count)
    nearby = (jnp.abs(bins_axis[:, None] - bins_axis[None, :]) <= HALF).astype(jnp.float32)
    return nearby / jnp.sum(nearby, axis=0, keepdims=True)


def lag_table(first_bin, bin_count):
    bins_axis = BAND_START + first_bin + lax.iota(jnp.int32, bin_count)
    shifts = jnp.mod(lax.iota(jnp.int32, LAGS) - LAGS // 2, SAMPLES)
    phase_index = jnp.mod(bins_axis[:, None] * shifts[None, :], SAMPLES)
    angles = phase_index.astype(jnp.float32) * (2.0 * math.pi / SAMPLES)
    return jnp.concatenate([jnp.cos(angles), -jnp.sin(angles)], axis=0).astype(jnp.bfloat16)


def pair_blocks(pair_offsets, pair_counts, pair_owner, block_count, slot_count):
    slot_index = lax.iota(jnp.int32, slot_count)
    starts = jnp.cumsum(pair_counts) - pair_counts
    first_block = jnp.sum((starts[None, :] <= slot_index[:, None]).astype(jnp.int32), axis=1) - 1
    member = lax.iota(jnp.int32, block_count)[None, :] == first_block[:, None]
    start_of = jnp.sum(jnp.where(member, starts[None, :], 0), axis=1)
    position = slot_index - start_of
    listed = jnp.sum(jnp.where(member[:, :, None], pair_offsets[None, :, :], 0), axis=1)
    chosen = lax.iota(jnp.int32, pair_offsets.shape[1])[None, :] == position[:, None]
    offset = jnp.sum(jnp.where(chosen, listed, 0), axis=1)
    second_block = jnp.mod(first_block + offset, block_count)
    held = pair_owner[None, :] == slot_index[:, None]
    slot_first = jnp.sum(jnp.where(held, first_block[None, :], 0), axis=1)
    slot_second = jnp.sum(jnp.where(held, second_block[None, :], 0), axis=1)
    return (slot_first, slot_second)


def cross_terms(first_spec, second_spec):
    turned = jnp.stack([first_spec[:, :, :, 1], -first_spec[:, :, :, 0]], axis=3)
    real_part = jnp.einsum(
        "tispf,tjspf->itjf", first_spec, second_spec, preferred_element_type=jnp.float32
    )
    imag_part = jnp.einsum(
        "tispf,tjspf->itjf", turned, second_spec, preferred_element_type=jnp.float32
    )
    return jnp.stack([real_part, imag_part], axis=3).astype(jnp.bfloat16)


def invert(spectra, table, norm_factor):
    flat = spectra.reshape(-1, spectra.shape[3] * spectra.shape[4])
    lagged = jnp.dot(flat, table, preferred_element_type=jnp.float32) * norm_factor
    return lagged.reshape(spectra.shape[:3] + (table.shape[1],))


def on_device(traces, pair_offsets, pair_counts, pair_owner):
    block_size, local_segs, sample_count = traces.shape
    parts_count = lax.axis_size("seg")
    block_count = lax.axis_size("chan")
    quarter_bins = FREQS // parts_count
    all_segs = local_segs * parts_count
    norm_factor = 1.0 / math.sqrt(FREQS * all_segs)
    signal = traces.reshape(block_size * local_segs, sample_count)
    width_bins = min(128, FREQS)
    pieces_count = FREQS // width_bins
    times_axis = lax.iota(jnp.int32, sample_count)

    def transform(piece_index):
        bins_axis = BAND_START + piece_index * width_bins + lax.iota(jnp.int32, width_bins)
        phase_index = jnp.mod(times_axis[:, None] * bins_axis[None, :], sample_count)
        angles = phase_index.astype(jnp.float32) * (2.0 * math.pi / sample_count)
        table_part = jnp.concatenate([jnp.cos(angles), -jnp.sin(angles)], axis=1)
        table_high = table_part.astype(jnp.bfloat16)
        table_low = (table_part - table_high.astype(jnp.float32)).astype(jnp.bfloat16)
        upper = jnp.dot(signal, table_high, preferred_element_type=jnp.float32)
        return upper + jnp.dot(signal, table_low, preferred_element_type=jnp.float32)

    spectrum = lax.map(transform, lax.iota(jnp.int32, pieces_count))
    spectrum = (
        spectrum.reshape(pieces_count, -1, 2, width_bins)
        .transpose(1, 2, 0, 3)
        .reshape(-1, 2, FREQS)
    )
    real_part = spectrum[:, 0]
    imag_part = spectrum[:, 1]
    amplitude = jnp.sqrt(real_part * real_part + imag_part * imag_part)
    smoothed = jnp.dot(
        amplitude,
        smoother(FREQS),
        precision=lax.Precision.HIGHEST,
        preferred_element_type=jnp.float32,
    )
    divisor = jnp.maximum(smoothed, 1.0)
    whitened = jnp.stack([real_part / divisor, imag_part / divisor], axis=1).astype(jnp.bfloat16)
    whitened = whitened.reshape(block_size, local_segs, 2, parts_count, quarter_bins)
    quarter = lax.all_to_all(whitened, "seg", split_axis=3, concat_axis=1, tiled=True)
    quarter = quarter.reshape(block_size, all_segs, 2, quarter_bins)
    slot_first, slot_second = pair_blocks(
        pair_offsets, pair_counts, pair_owner, block_count, TILE_DEV * block_count
    )
    my_start = lax.axis_index("chan") * TILE_DEV
    needed = jnp.concatenate(
        [
            lax.dynamic_slice_in_dim(slot_first, my_start, TILE_DEV),
            lax.dynamic_slice_in_dim(slot_second, my_start, TILE_DEV),
        ]
    )
    empty_blocks = jnp.zeros((2 * TILE_DEV, block_size, all_segs, 2, quarter_bins), jnp.bfloat16)
    incoming = lax.all_gather(quarter, "chan", axis=0, tiled=True)
    block_total = incoming.shape[0] // block_size
    incoming_blocks = incoming.reshape(block_total, block_size, all_segs, 2, quarter_bins)
    inside = (needed >= 0) & (needed < block_total)
    picked = jnp.take(incoming_blocks, jnp.clip(needed, 0, block_total - 1), axis=0)
    held_blocks = jnp.where(inside[:, None, None, None, None], picked, empty_blocks)
    first_spec = held_blocks[:TILE_DEV]
    second_spec = held_blocks[TILE_DEV:]
    full_table = lag_table(0, FREQS)
    spectra = cross_terms(first_spec, second_spec)
    return invert(
        lax.all_to_all(spectra, "seg", split_axis=0, concat_axis=4, tiled=True),
        full_table,
        norm_factor,
    )


def solution(mesh):
    placed = (P("chan", "seg", None), P(), P(), P())
    return jax.shard_map(
        on_device,
        mesh=mesh,
        in_specs=placed,
        out_specs=P("seg", "chan", None, None),
        check_vma=False,
    )
```

profile of v0, /device:TPU:1, one launch (start us, length us, event | category | flops | bytes accessed | tf_op | source)
XLA Modules:
  0.0 654.8 jit_solution(10971345784729674654)
XLA Ops:
  6.6 7.2 %reshape.215 = bf16[256,8192]{1,0:T(8,128)(2,1)} reshape(bf16[128,2,8192]{2,1,0:T(2,128)(2,1)} %param.6) | data formatting | bytes 8388608 | tf_op jit(solution)/shard_map/reshape | solution.py:71
  13.8 82.4 %while.13 = (s32[]{:T(128)}, f32[4,256,256]{1,2,0:T(8,128)S(1)}, s32[4]{0:T(128)S(1)}, bf16[256,8192]{1,0:T(8,128)(2,1)}, s32[]{:T(128)}, /*index=5*/s32[1]{0:T(128)}, s32[1]{0:T(128)}) while((s32[]{:T(128)}, f32[4,256,256]{1,2,0:T(8,128)S(1)}, s32[4]{0:T(128)S(1)}, bf16[256,8192]{1,0:T(8,128)(2,1)}, s32[]{:T(128)}, ...), condition=%wide.region_8.9_spmd.clone, body=%wide.region_7.8_spmd.clone.sunk | while | flops 2182152192 | bytes 51119252 | solution.py:86
  15.2 16.5 %fusion.57 = (f32[8192,128]{1,0:T(8,128)S(1)}, f32[8192,128]{1,0:T(8,128)S(1)}) fusion(s32[128]{0:T(128)S(1)} %iota_add_fusion.3), kind=kLoop, calls=%fused_computation.18.clone.1 | loop fusion | flops 15728640 | bytes 8389120 | tf_op jit(solution)/shard_map/while/body/eval_jaxpr/cos | solution.py:80
  31.7 1.3 fusion.58
  33.0 1.3 fusion.59
  34.4 0.7 dynamic_slice.19
  35.7 16.5 %fusion.57 = (f32[8192,128]{1,0:T(8,128)S(1)}, f32[8192,128]{1,0:T(8,128)S(1)}) fusion(s32[128]{0:T(128)S(1)} %iota_add_fusion.3), kind=kLoop, calls=%fused_computation.18.clone.1 | loop fusion | flops 15728640 | bytes 8389120 | tf_op jit(solution)/shard_map/while/body/eval_jaxpr/cos | solution.py:80
  52.3 1.3 fusion.58
  53.6 1.3 fusion.59
  54.9 0.7 dynamic_slice.19
  56.3 16.5 %fusion.57 = (f32[8192,128]{1,0:T(8,128)S(1)}, f32[8192,128]{1,0:T(8,128)S(1)}) fusion(s32[128]{0:T(128)S(1)} %iota_add_fusion.3), kind=kLoop, calls=%fused_computation.18.clone.1 | loop fusion | flops 15728640 | bytes 8389120 | tf_op jit(solution)/shard_map/while/body/eval_jaxpr/cos | solution.py:80
  72.8 1.3 fusion.58
  74.1 1.3 fusion.59
  76.8 16.5 %fusion.57 = (f32[8192,128]{1,0:T(8,128)S(1)}, f32[8192,128]{1,0:T(8,128)S(1)}) fusion(s32[128]{0:T(128)S(1)} %iota_add_fusion.3), kind=kLoop, calls=%fused_computation.18.clone.1 | loop fusion | flops 15728640 | bytes 8389120 | tf_op jit(solution)/shard_map/while/body/eval_jaxpr/cos | solution.py:80
  93.4 1.3 fusion.58
  94.7 1.3 fusion.59
  97.0 1.2 divide_convert_fusion.1
  98.6 19.0 %all_to_all.30 = bf16[128,2,2,4,128]{4,0,2,1,3:T(8,128)(2,1)} all-to-all(bf16[128,2,2,4,128]{4,0,2,1,3:T(8,128)(2,1)S(1)} %pad_maximum_fusion.2), channel_id=1, replica_groups=mesh['chan'=8,'seg'=4] {'seg'}, dimensions={3} | all-to-all | bytes 1048576 | tf_op jit(solution)/shard_map/all_to_all | solution.py:104
  118.8 36.3 %all-gather.2.cloned.1.call-done = bf16[1024,8,2,128]{3,0,2,1:T(8,128)(2,1)} async-done(((bf16[128,8,2,128]{3,0,2,1:T(8,128)(2,1)}), bf16[1024,8,2,128]{3,0,2,1:T(8,128)(2,1)}) %all-gather.2.cloned.1.call-update) | async-done | bytes 4194320 | tf_op jit(solution)/shard_map/all_gather | solution.py:117
  155.1 6.9 %copy.25 = bf16[1024,8,2,128]{3,1,2,0:T(8,128)(2,1)} copy(bf16[1024,8,2,128]{3,0,2,1:T(8,128)(2,1)} %all-gather.2.cloned.1.call-done) | data formatting | bytes 8388608 | tf_op jit(solution)/shard_map/all_gather | solution.py:117
  162.0 4.4 gather_fusion
  166.3 4.2 copy.26
  171.0 4.9 fusion.18
  175.9 4.9 fusion.19
  180.8 6.8 %pad_maximum_fusion.1 = bf16[128,2,128,2,128]{0,2,4,1,3:T(8,128)(2,1)} fusion(bf16[128,2,128,1,128]{0,2,4,1,3:T(8,128)(2,1)S(1)} %fusion.19, bf16[128,2,128,1,128]{0,2,4,1,3:T(8,128)(2,1)S(1)} %fusion.18), kind=kLoop, calls=%fused_computation.25 | loop fusion | flops 8388608 | bytes 33554432 | tf_op jit(solution)/shard_map/stack | solution.py:55
  187.6 23.5 %copy.27 = bf16[128,2,128,2,128]{2,4,1,3,0:T(8,128)(2,1)} copy(bf16[128,2,128,2,128]{0,2,4,1,3:T(8,128)(2,1)} %pad_maximum_fusion.1) | data formatting | bytes 33554432 | tf_op jit(solution)/shard_map/stack | solution.py:55
  211.1 7.2 %all-to-all-start.1 = ((bf16[128,2,128,2,128]{2,4,1,3,0:T(8,128)(2,1)}), bf16[128,2,128,2,128]{2,4,1,3,0:T(8,128)(2,1)}, u32[]{:S(2)}, u32[]{:S(2)}) async-start(bf16[128,2,128,2,128]{2,4,1,3,0:T(8,128)(2,1)} %copy.27), calls=%async_computation.1 | async-start | bytes 33554432 | tf_op jit(solution)/shard_map/all_to_all | solution.py:128
  218.3 2.5 cosine_convert_fusion
  220.8 360.1 %all-to-all-done.1 = bf16[128,2,128,2,128]{2,4,1,3,0:T(8,128)(2,1)} async-done(((bf16[128,2,128,2,128]{2,4,1,3,0:T(8,128)(2,1)}), bf16[128,2,128,2,128]{2,4,1,3,0:T(8,128)(2,1)}, u32[]{:S(2)}, u32[]{:S(2)}) %all-to-all-start.1) | async-done | bytes 16777248 | tf_op jit(solution)/shard_map/all_to_all | solution.py:128
  580.9 26.0 %copy.29 = bf16[32,2,128,2,4,128]{5,4,3,2,1,0:T(4,128)(2,1)} copy(bf16[32,2,128,2,4,128]{2,5,1,3,0,4:T(8,128)(2,1)} %bitcast.23) | data formatting | bytes 33554432 | tf_op jit(solution)/shard_map/all_to_all | solution.py:128
  606.9 27.3 %reshape.220 = bf16[8192,1024]{1,0:T(8,128)(2,1)} reshape(bf16[32,2,128,2,4,128]{5,4,3,2,1,0:T(4,128)(2,1)} %copy.29) | data formatting | bytes 33554432 | tf_op jit(solution)/shard_map/reshape | solution.py:59
  634.3 13.7 %convolution_multiply_fusion = f32[8192,256]{1,0:T(8,128)} fusion(bf16[8192,1024]{1,0:T(8,128)(2,1)} %reshape.220, bf16[512,256]{1,0:T(8,128)(2,1)S(1)} %get-tuple-element.99, bf16[512,256]{1,0:T(8,128)(2,1)S(1)} %get-tuple-element.98), kind=kOutput, calls=%fused_computation.28 | convolution fusion | flops 4298113024 | bytes 25690112 | tf_op jit(solution)/shard_map/dot_general | solution.py:60
  (55 shorter events, 4.2 us)
Async XLA Ops:
  6.5 148.6 %all-gather.2.cloned.1.call-start = ((), (), s32[]{:S(2)}) async-start(), calls=%async_computation.2 | async-start | bytes 4718592 | tf_op jit(solution)/shard_map/all_gather | solution.py:117
  15.2 16.5 %copy-start = (bf16[256,8192]{1,0:T(8,128)(2,1)S(1)}, bf16[256,8192]{1,0:T(8,128)(2,1)}, u32[]{:S(2)}) copy-start(bf16[256,8192]{1,0:T(8,128)(2,1)} %get-tuple-element.148) | copy-start | bytes 12582916 | tf_op jit(solution)/shard_map/while
  35.7 16.5 %copy-start = (bf16[256,8192]{1,0:T(8,128)(2,1)S(1)}, bf16[256,8192]{1,0:T(8,128)(2,1)}, u32[]{:S(2)}) copy-start(bf16[256,8192]{1,0:T(8,128)(2,1)} %get-tuple-element.148) | copy-start | bytes 12582916 | tf_op jit(solution)/shard_map/while
  56.3 16.5 %copy-start = (bf16[256,8192]{1,0:T(8,128)(2,1)S(1)}, bf16[256,8192]{1,0:T(8,128)(2,1)}, u32[]{:S(2)}) copy-start(bf16[256,8192]{1,0:T(8,128)(2,1)} %get-tuple-element.148) | copy-start | bytes 12582916 | tf_op jit(solution)/shard_map/while
  76.8 16.5 %copy-start = (bf16[256,8192]{1,0:T(8,128)(2,1)S(1)}, bf16[256,8192]{1,0:T(8,128)(2,1)}, u32[]{:S(2)}) copy-start(bf16[256,8192]{1,0:T(8,128)(2,1)} %get-tuple-element.148) | copy-start | bytes 12582916 | tf_op jit(solution)/shard_map/while
  98.2 19.3 %copy-start.3 = (s32[8]{0:T(128)S(1)}, s32[8]{0:T(128)}, u32[]{:S(2)}) copy-start(s32[8]{0:T(128)} %param.8) | copy-start | bytes 100
  98.2 19.5 %copy-start.1 = (s32[8,7]{1,0:T(8,128)S(1)}, s32[8,7]{1,0:T(8,128)}, u32[]{:S(2)}) copy-start(s32[8,7]{1,0:T(8,128)} %param.7) | copy-start | bytes 676
  98.3 19.9 %copy-start.2 = (s32[16]{0:T(128)S(1)}, s32[16]{0:T(128)}, u32[]{:S(2)}) copy-start(s32[16]{0:T(128)} %param.9) | copy-start | bytes 196
  211.1 369.8 %all-to-all-start.1 = ((bf16[128,2,128,2,128]{2,4,1,3,0:T(8,128)(2,1)}), bf16[128,2,128,2,128]{2,4,1,3,0:T(8,128)(2,1)}, u32[]{:S(2)}, u32[]{:S(2)}) async-start(bf16[128,2,128,2,128]{2,4,1,3,0:T(8,128)(2,1)} %copy.27), calls=%async_computation.1 | async-start | bytes 33554432 | tf_op jit(solution)/shard_map/all_to_all | solution.py:128
Sparse Core Ops, SparseCore 0:
  117.7 37.3 all-gather.1
where the time goes:
time: 658 us; the launch traced here: 655 us
  waiting for transfers between devices  396 us (60%)
  local copies, waits for them, and re-layouts  104 us (16%)
  other arithmetic  76.8 us (12%)
  matrix products  35.1 us (5%)
  blocking collectives  19 us (3%)
  between operations  13.6 us (2%)
  starting transfers between devices  7.18 us (1%)
    all_to_all x1, waiting for transfers between devices, on_device(): lax.all_to_all(spectra, 'seg', split_axis=0, concat_axis=4, tiled=True)  360 us
    cos x4, other arithmetic, transform(): table_part = jnp.concatenate([jnp.cos(angles), -jnp.sin(angles)], axis=1)  66.1 us
    all_gather x1, waiting for transfers between devices, on_device(): incoming = lax.all_gather(quarter, 'chan', axis=0, tiled=True)  36.3 us
    reshape x1, local copies, waits for them, and re-layouts, invert(): flat = spectra.reshape(-1, spectra.shape[3] * spectra.shape[4])  27.3 us
    all_to_all x1, local copies, waits for them, and re-layouts, on_device(): lax.all_to_all(spectra, 'seg', split_axis=0, concat_axis=4, tiled=True)  26 us
    another operation x1, local copies, waits for them, and re-layouts, cross_terms(): return jnp.stack([real_part, imag_part], axis=3).astype(jnp.bfloat16)  23.5 us
    all_to_all x1, blocking collectives, on_device(): lax.all_to_all(whitened, 'seg', split_axis=3, concat_axis=1, tiled=True)  19 us
    dot_general x1, matrix products, invert(): jnp.dot(flat, table, preferred_element_type=jnp.float32) * norm_factor  13.7 us
  transfers between devices with their start and end apart: 2, of which 2 were waited for; matrix products, arithmetic and copies ran while one was open for 1% of the time, Pallas kernels for 0%

commit v1 on v0

v1 whole, which is shorter than its diff:
```python
import functools
import math

import jax
import jax.numpy as jnp
import ml_dtypes
import numpy as np
from jax import lax
from jax.experimental import pallas as pl
from jax.experimental.pallas import tpu as pltpu
from jax.sharding import PartitionSpec as P

SAMPLES = 8192
BAND_START = 32
FREQS = 512
HALF = 8
LAGS = 256
TILE_DEV = 2

RADIX = 8
FOLDED = SAMPLES // RADIX
RESIDUES = (0, 4, 1, 7, 2, 6, 3, 5)
PER_RES = FREQS // RADIX
CHUNK = 256
STEPS = FOLDED // CHUNK
BF16 = ml_dtypes.bfloat16

BIN_ORDER = np.concatenate([np.arange(PER_RES) * RADIX + r for r in RESIDUES])


def dft_tables():
    n = np.arange(FOLDED)
    full = np.zeros((4, 4 * PER_RES, 2, FOLDED))
    for group in range(4):
        first, second = RESIDUES[2 * group], RESIDUES[2 * group + 1]
        parts = []
        for r in (first, second):
            k = BAND_START + np.arange(PER_RES) * RADIX + r
            angle = 2.0 * np.pi / SAMPLES * ((k[:, None] * n[None, :]) % SAMPLES)
            parts.append((np.cos(angle), np.sin(angle)))
        (c0, s0), (c1, s1) = parts
        o = np.zeros_like(c0)
        if group == 0:
            rows = [(c0, o), (-s0, o), (o, c1), (o, -s1)]
        else:
            rows = [(c0, s0), (-s0, c0), (c1, -s1), (-s1, -c1)]
        for i, (a, b) in enumerate(rows):
            full[group, i * PER_RES:(i + 1) * PER_RES, 0] = a
            full[group, i * PER_RES:(i + 1) * PER_RES, 1] = b
    full = full.reshape(4, 4 * PER_RES, 2, STEPS, CHUNK).transpose(3, 0, 1, 2, 4)
    full = full.reshape(STEPS, 4, 4 * PER_RES, 2 * CHUNK).astype(np.float32)
    high = full.astype(BF16)
    low = (full - high.astype(np.float32)).astype(BF16)
    return high, low


def lag_table():
    shifts = np.arange(LAGS) - LAGS // 2
    angle = 2.0 * np.pi / SAMPLES * (((BAND_START + BIN_ORDER)[None, :] * shifts[:, None]) % SAMPLES)
    return np.concatenate([np.cos(angle), -np.sin(angle)], axis=1).astype(np.float32).astype(BF16)


def window_tables():
    near = np.abs(BIN_ORDER[:, None] - BIN_ORDER[None, :]) <= HALF
    count = near.sum(axis=1).astype(np.float32)
    return near.astype(BF16), np.ascontiguousarray(np.broadcast_to(count[:, None], (FREQS, 256)))


def split(value):
    high = value.astype(jnp.bfloat16)
    return high, (value - high.astype(jnp.float32)).astype(jnp.bfloat16)


def dot_nt(a, b):
    return lax.dot_general(a, b, (((1,), (1,)), ((), ())), preferred_element_type=jnp.float32)


def dot_nn(a, b):
    return jnp.dot(a, b, preferred_element_type=jnp.float32)


def whiten_kernel(*refs):
    xs = refs[:RADIX]
    high_ref, low_ref, near_ref, count_ref, perm_ref, out_ref, total = refs[RADIX:]
    step = pl.program_id(0)

    @pl.when(step == 0)
    def _():
        total[...] = jnp.zeros_like(total)

    x = [ref[...].astype(jnp.float32) for ref in xs]
    e0, e1, e2, e3 = x[0] + x[4], x[1] + x[5], x[2] + x[6], x[3] + x[7]
    d0, d1, d2, d3 = x[0] - x[4], x[1] - x[5], x[2] - x[6], x[3] - x[7]
    root = math.sqrt(0.5)
    plus, minus = (d1 + d3) * root, (d1 - d3) * root
    folded = (
        ((e0 + e2) + (e1 + e3), (e0 + e2) - (e1 + e3)),
        (d0 + minus, -(d2 + plus)),
        (e0 - e2, e3 - e1),
        (d0 - minus, d2 - plus),
    )
    for group, (a, b) in enumerate(folded):
        a_high, a_low = split(a)
        b_high, b_low = split(b)
        y_high = jnp.concatenate([a_high, b_high], axis=1)
        y_low = jnp.concatenate([a_low, b_low], axis=1)
        t_high = high_ref[0, group]
        part = dot_nt(t_high, y_high) + dot_nt(t_high, y_low) + dot_nt(low_ref[0, group], y_high)
        total[group] += part

    @pl.when(step == STEPS - 1)
    def _():
        real, imag = [], []
        for group in range(4):
            for half in range(2):
                base = half * 2 * PER_RES
                real.append(total[group, base:base + PER_RES])
                imag.append(total[group, base + PER_RES:base + 2 * PER_RES])
        real = jnp.concatenate(real, axis=0)
        imag = jnp.concatenate(imag, axis=0)
        amplitude = jnp.sqrt(real * real + imag * imag)
        high, rest = amplitude.astype(jnp.bfloat16), None
        rest = amplitude - high.astype(jnp.float32)
        mid, low = split(rest)
        near = near_ref[...]
        summed = dot_nn(near, high) + (dot_nn(near, mid) + dot_nn(near, low))
        divisor = jnp.maximum(summed / count_ref[...], 1.0)
        segs = out_ref.shape[0]
        for part, value in enumerate((real, imag)):
            white = (value / divisor).astype(jnp.bfloat16)
            moved = dot_nn(white, perm_ref[...]).astype(jnp.bfloat16)
            width = moved.shape[1] // segs
            for s in range(segs):
                out_ref[s, part] = moved[:, s * width:(s + 1) * width]


def whiten(signal, block_size, segs):
    rows = block_size * segs
    high, low = dft_tables()
    near, count = window_tables()
    perm = np.zeros((rows, rows), np.float32)
    for c in range(block_size):
        for s in range(segs):
            perm[c * segs + s, s * block_size + c] = 1.0
    once = lambda shape: pl.BlockSpec(shape, lambda q: (0,) * len(shape))
    table = pl.BlockSpec((1, 4, 4 * PER_RES, 2 * CHUNK), lambda q: (q, 0, 0, 0))
    return pl.pallas_call(
        whiten_kernel,
        grid=(STEPS,),
        in_specs=[
            pl.BlockSpec((rows, CHUNK), functools.partial(lambda j, q: (0, j * STEPS + q), j))
            for j in range(RADIX)
        ] + [table, table, once((FREQS, FREQS)), once((FREQS, 256)), once((rows, rows))],
        out_specs=once((segs, 2, FREQS, block_size)),
        out_shape=jax.ShapeDtypeStruct((segs, 2, FREQS, block_size), jnp.bfloat16),
        scratch_shapes=[pltpu.VMEM((4, 4 * PER_RES, rows), jnp.float32)],
        compiler_params=pltpu.CompilerParams(vmem_limit_bytes=48 << 20),
    )(*([signal] * RADIX), jnp.asarray(high), jnp.asarray(low), jnp.asarray(near),
      jnp.asarray(count[:, :rows]), jnp.asarray(perm.astype(BF16)))


GROUP = 16
FCHUNK = 64
CROSS_STEPS = FREQS // FCHUNK
ROWS_STEP = 4


def stack_kernel(norm_factor, parts, segs, rows, index_ref, first_ref, second_ref, table_ref, out_ref, cross):
    step = pl.program_id(1)
    depth = parts * segs * 2 * GROUP
    block = second_ref.shape[-1]

    @pl.when(step < CROSS_STEPS)
    def _():
        own = index_ref[4] * rows
        select = (
            lax.broadcasted_iota(jnp.int32, (rows, block), 1)
            == lax.broadcasted_iota(jnp.int32, (rows, block), 0) + own
        ).astype(jnp.bfloat16)
        mask = (
            lax.broadcasted_iota(jnp.int32, (rows, GROUP, depth), 2) % GROUP
            == lax.broadcasted_iota(jnp.int32, (rows, GROUP, depth), 1)
        )
        for g in range(FCHUNK // GROUP):
            span = slice(g * GROUP, (g + 1) * GROUP)
            firsts, plain, turned = [], [], []
            for z in range(parts):
                for s in range(segs):
                    firsts += [first_ref[0, z, s, p, span] for p in range(2)]
                    re, im = second_ref[0, z, s, 0, span], second_ref[0, z, s, 1, span]
                    plain += [re, im]
                    turned += [-im, re]
            left = dot_nt(select, jnp.concatenate(firsts, axis=0))
            wide = jnp.broadcast_to(left[:, None, :], (rows, GROUP, depth))
            wide = jnp.where(mask, wide, 0.0).reshape(rows * GROUP, depth).astype(jnp.bfloat16)
            right = jnp.concatenate(
                [jnp.concatenate(plain, axis=0), jnp.concatenate(turned, axis=0)], axis=1
            )
            result = dot_nn(wide, right).astype(jnp.bfloat16).reshape(rows, GROUP, 2 * block)
            at = pl.multiple_of(step * FCHUNK + g * GROUP, GROUP)
            cross[:, 0, pl.ds(at, GROUP), :] = result[:, :, :block]
            cross[:, 1, pl.ds(at, GROUP), :] = result[:, :, block:]

    @pl.when(step >= CROSS_STEPS)
    def _():
        base = (step - CROSS_STEPS) * ROWS_STEP
        table = table_ref[...]
        for pair in range(ROWS_STEP // 2):
            both = [
                cross[base + 2 * pair + h].reshape(2 * FREQS, block) for h in range(2)
            ]
            lagged = dot_nn(table, jnp.concatenate(both, axis=1)) * norm_factor
            for h in range(2):
                out_ref[2 * pair + h, 0] = lagged[:, h * block:(h + 1) * block].T


def stack(index, gathered, norm_factor, rows):
    _, parts, segs, _, _, block = gathered.shape
    grid = (TILE_DEV, CROSS_STEPS + rows // ROWS_STEP)
    shape = (1, parts, segs, 2, FCHUNK, block)

    def place(offset, slot, step, index_ref):
        return (index_ref[offset + slot], 0, 0, 0, jnp.minimum(step, CROSS_STEPS - 1), 0)

    return pl.pallas_call(
        functools.partial(stack_kernel, norm_factor, parts, segs, rows),
        grid_spec=pltpu.PrefetchScalarGridSpec(
            num_scalar_prefetch=1,
            grid=grid,
            in_specs=[
                pl.BlockSpec(shape, functools.partial(place, 0)),
                pl.BlockSpec(shape, functools.partial(place, TILE_DEV)),
                pl.BlockSpec((LAGS, 2 * FREQS), lambda slot, step, index_ref: (0, 0)),
            ],
            out_specs=pl.BlockSpec(
                (ROWS_STEP, 1, block, LAGS),
                lambda slot, step, index_ref: (jnp.maximum(step - CROSS_STEPS, 0), slot, 0, 0),
            ),
            scratch_shapes=[pltpu.VMEM((rows, 2, FREQS, block), jnp.bfloat16)],
        ),
        out_shape=jax.ShapeDtypeStruct((rows, TILE_DEV, block, LAGS), jnp.float32),
        compiler_params=pltpu.CompilerParams(vmem_limit_bytes=48 << 20),
    )(index, gathered, gathered, jnp.asarray(lag_table()))


def pair_blocks(pair_offsets, pair_counts, pair_owner, block_count, slot_count):
    slot_index = lax.iota(jnp.int32, slot_count)
    starts = jnp.cumsum(pair_counts) - pair_counts
    first_block = jnp.sum((starts[None, :] <= slot_index[:, None]).astype(jnp.int32), axis=1) - 1
    member = lax.iota(jnp.int32, block_count)[None, :] == first_block[:, None]
    start_of = jnp.sum(jnp.where(member, starts[None, :], 0), axis=1)
    position = slot_index - start_of
    listed = jnp.sum(jnp.where(member[:, :, None], pair_offsets[None, :, :], 0), axis=1)
    chosen = lax.iota(jnp.int32, pair_offsets.shape[1])[None, :] == position[:, None]
    offset = jnp.sum(jnp.where(chosen, listed, 0), axis=1)
    second_block = jnp.mod(first_block + offset, block_count)
    held = pair_owner[None, :] == slot_index[:, None]
    slot_first = jnp.sum(jnp.where(held, first_block[None, :], 0), axis=1)
    slot_second = jnp.sum(jnp.where(held, second_block[None, :], 0), axis=1)
    return (slot_first, slot_second)


def on_device(traces, pair_offsets, pair_counts, pair_owner):
    block_size, local_segs, sample_count = traces.shape
    parts_count = lax.axis_size("seg")
    block_count = lax.axis_size("chan")
    norm_factor = 1.0 / math.sqrt(FREQS * local_segs * parts_count)
    signal = traces.reshape(block_size * local_segs, sample_count)
    whitened = whiten(signal, block_size, local_segs)
    gathered = lax.all_gather(lax.all_gather(whitened, "seg", axis=0), "chan", axis=0)
    slot_first, slot_second = pair_blocks(
        pair_offsets, pair_counts, pair_owner, block_count, pair_owner.shape[0]
    )
    my_start = lax.axis_index("chan") * TILE_DEV
    index = jnp.concatenate(
        [
            lax.dynamic_slice_in_dim(slot_first, my_start, TILE_DEV),
            lax.dynamic_slice_in_dim(slot_second, my_start, TILE_DEV),
            lax.axis_index("seg")[None],
        ]
    ).astype(jnp.int32)
    return stack(index, gathered, norm_factor, block_size // parts_count)


def solution(mesh):
    placed = (P("chan", "seg", None), P(), P(), P())
    return jax.shard_map(
        on_device,
        mesh=mesh,
        in_specs=placed,
        out_specs=P("seg", "chan", None, None),
        check_vma=False,
    )
```

time: 658 us -> 201 us (0.31)
  waiting for transfers between devices: 396 us -> 138 us
  local copies, waits for them, and re-layouts: 104 us -> 9.7 us
  other arithmetic: 76.8 us -> 0.69 us
  Pallas kernels: 0 us -> 38 us
  matrix products: 35.1 us -> 0 us
  blocking collectives: 19 us -> 0 us
  starting transfers between devices: 7.18 us -> 0.04 us
    all_to_all x1 -> x0, waiting for transfers between devices: 360 us -> none  [on_device(): lax.all_to_all(spectra, 'seg', split_axis=0, concat_axis=4, tiled=True)]
    all_gather x1 -> x2, waiting for transfers between devices: 36.3 us -> 138 us  [the longest x1 89.9 us: on_device(): lax.all_gather(lax.all_gather(whitened, 'seg', axis=0), 'chan', axis=0)]
    cos x4 -> x0, other arithmetic: 66.1 us -> none  [transform(): table_part = jnp.concatenate([jnp.cos(angles), -jnp.sin(angles)], axis=1)]
    pallas_call x0 -> x2, Pallas kernels: none -> 38 us  [the longest x1 28.5 us: stack(): pl.pallas_call(functools.partial(stack_kernel, norm_factor, parts, segs,...]
    dot_general x12 -> x0, matrix products: 35.1 us -> none  [the longest x1 13.7 us: invert(): jnp.dot(flat, table, preferred_element_type=jnp.float32) * norm_factor]
    reshape x3 -> x0, local copies, waits for them, and re-layouts: 28.1 us -> none  [the longest x1 27.3 us: invert(): flat = spectra.reshape(-1, spectra.shape[3] * spectra.shape[4])]
    all_to_all x1 -> x0, local copies, waits for them, and re-layouts: 26 us -> none  [on_device(): lax.all_to_all(spectra, 'seg', split_axis=0, concat_axis=4, tiled=True)]
    another operation x5 -> x0, local copies, waits for them, and re-layouts: 23.7 us -> none  [the longest x1 23.5 us: cross_terms(): return jnp.stack([real_part, imag_part], axis=3).astype(jnp.bfloat16)]
  transfers between devices with their start and end apart: 2 -> 2, of which waited for: 2 -> 2; matrix products, arithmetic and copies ran while one was open for 1% -> 0% of each run, Pallas kernels for 0% -> 0%
where the time goes in v1:
time: 201 us; the launch traced here: 200 us
  waiting for transfers between devices  138 us (69%)
  Pallas kernels  38 us (19%)
  between operations  13.5 us (7%)
  local copies, waits for them, and re-layouts  9.7 us (5%)
    all_gather x1, waiting for transfers between devices, on_device(): lax.all_gather(lax.all_gather(whitened, 'seg', axis=0), 'chan', axis=0)  89.9 us
    all_gather x1, waiting for transfers between devices, on_device(): lax.all_gather(whitened, 'seg', axis=0)  48.1 us
    pallas_call x1, Pallas kernels, stack(): pl.pallas_call(functools.partial(stack_kernel, norm_factor, parts, segs,...  28.5 us
    pallas_call x1, Pallas kernels, whiten(): pl.pallas_call(whiten_kernel, grid=(STEPS,), in_specs=[pl.BlockSpec((rows...  9.56 us
    reshape x1, local copies, waits for them, and re-layouts, on_device(): signal = traces.reshape(block_size * local_segs, sample_count)  7.26 us
  transfers between devices with their start and end apart: 2, of which 2 were waited for; matrix products, arithmetic and copies ran while one was open for 0% of the time, Pallas kernels for 0%

profile of v1, /device:TPU:1, one launch (start us, length us, event | category | flops | bytes accessed | tf_op | source)
XLA Modules:
  0.0 200.0 jit_solution(2771962451128273036)
XLA Ops:
  6.5 0.0 copy-start.2
  6.5 0.0 copy-start.3
  6.5 0.0 copy-start.4
  6.5 0.0 all-gather.5.cloned.1.call-start
  6.5 7.3 %reshape.82.refs_0_.refs_1_.refs_2_.refs_3_.refs_4_.refs_5_.refs_6_.refs_7_ = bf16[256,8192]{1,0:T(8,128)(2,1)} reshape(bf16[128,2,8192]{2,1,0:T(2,128)(2,1)} %param.10) | data formatting | bytes 8388608 | tf_op jit(solution)/shard_map/reshape | solution.py:268
  13.8 0.0 copy-done.2
  13.8 0.0 copy-done.3
  13.8 0.0 copy-done.4
  13.8 0.0 copy-start
  13.8 2.2 %copy-done = bf16[256,8192]{1,0:T(8,128)(2,1)S(1)} copy-done((bf16[256,8192]{1,0:T(8,128)(2,1)S(1)}, bf16[256,8192]{1,0:T(8,128)(2,1)}, u32[]{:S(2)}) %copy-start) | copy-done | bytes 4194328
  16.0 0.0 copy-start.7
  16.0 0.0 copy-start.6
  16.0 9.6 %shard_map.100 = bf16[2,2,512,128]{3,2,1,0:T(8,128)(2,1)} custom-call(bf16[256,8192]{1,0:T(8,128)(2,1)S(1)} %copy-done, bf16[256,8192]{1,0:T(8,128)(2,1)S(1)} %copy-done, bf16[256,8192]{1,0:T(8,128)(2,1)S(1)} %copy-done, bf16[256,8192]{1,0:T(8,128)(2,1)S(1)} %copy-done, bf16[256,8192]{1,0:T(8,128)(2,1)S(1)} %copy-done, bf16[256,8192]{1,0:T(8,128)(2,1)S(1)} %copy-done, ...), custom_call_target="tpu_custom_call" | custom-call | tf_op jit(solution)/shard_map/pallas_call | solution.py:147
  25.6 0.0 all-gather.5.cloned.1.call-update
  25.6 0.0 all-gather.7.cloned.1.call-start
  25.7 48.1 %all-gather.5.cloned.1.call-done = bf16[8,2,512,128]{3,2,1,0:T(8,128)(2,1)} async-done(((bf16[2,2,512,128]{3,2,1,0:T(8,128)(2,1)}), bf16[8,2,512,128]{3,2,1,0:T(8,128)(2,1)}) %all-gather.5.cloned.1.call-update) | async-done | bytes 2097168 | tf_op jit(solution)/shard_map/all_gather | solution.py:270
  73.8 0.0 all-gather.7.cloned.1.call-update
  73.8 0.0 copy-done.7
  73.8 0.2 reduce-window.9
  74.0 0.0 copy-done.5
  74.0 0.1 copy.11
  74.1 0.1 convert_reduce_fusion
  74.2 0.1 select_reduce_fusion.4
  74.3 0.1 select_reduce_fusion
  74.4 0.0 copy-done.6
  74.4 0.1 select_reduce_fusion.2
  74.5 0.1 dynamic_slice.6
  74.6 0.1 dynamic_slice.7
  74.7 0.1 pad_add_fusion.index_ref
  74.8 89.9 %all-gather.7.cloned.1.call-done = bf16[32,2,2,512,128]{4,3,2,1,0:T(8,128)(2,1)} async-done(((bf16[4,2,2,512,128]{4,3,2,1,0:T(8,128)(2,1)}), bf16[32,2,2,512,128]{4,3,2,1,0:T(8,128)(2,1)}) %all-gather.7.cloned.1.call-update) | async-done | bytes 16777232 | tf_op jit(solution)/shard_map/all_gather | solution.py:270
  164.7 0.0 copy-done.1
  164.7 28.5 %shard_map.101 = f32[32,2,128,256]{3,2,1,0:T(8,128)} custom-call(s32[5]{0:T(128)S(1)} %pad_add_fusion.index_ref, bf16[8,4,2,2,512,128]{5,4,3,2,1,0:T(8,128)(2,1)} %bitcast.6, bf16[8,4,2,2,512,128]{5,4,3,2,1,0:T(8,128)(2,1)} %bitcast.7, bf16[256,1024]{1,0:T(8,128)(2,1)S(1)} %copy-done.1), custom_call_target="tpu_custom_call" | custom-call | tf_op jit(solution)/shard_map/pallas_call | solution.py:225
  (8 shorter events, 0.1 us)
Async XLA Ops:
  6.5 7.3 %copy-start.2 = (f32[512,256]{1,0:T(8,128)S(1)}, f32[512,256]{1,0:T(8,128)}, u32[]{:S(2)}) copy-start(f32[512,256]{1,0:T(8,128)} %constant.50.clone.refs_11_) | copy-start | bytes 1572868
  6.5 7.3 %copy-start.3 = (bf16[512,512]{1,0:T(8,128)(2,1)S(1)}, bf16[512,512]{1,0:T(8,128)(2,1)}, u32[]{:S(2)}) copy-start(bf16[512,512]{1,0:T(8,128)(2,1)} %constant.49.clone.refs_10_) | copy-start | bytes 1572868
  6.5 7.3 %copy-start.4 = (bf16[256,256]{1,0:T(8,128)(2,1)S(1)}, bf16[256,256]{1,0:T(8,128)(2,1)}, u32[]{:S(2)}) copy-start(bf16[256,256]{1,0:T(8,128)(2,1)} %constant.51.clone.refs_12_) | copy-start | bytes 393220
  6.5 67.2 %all-gather.5.cloned.1.call-start = ((), (), s32[]{:S(2)}) async-start(), calls=%async_computation | async-start | bytes 2621440 | tf_op jit(solution)/shard_map/all_gather | solution.py:270
  13.8 2.2 %copy-start = (bf16[256,8192]{1,0:T(8,128)(2,1)S(1)}, bf16[256,8192]{1,0:T(8,128)(2,1)}, u32[]{:S(2)}) copy-start(bf16[256,8192]{1,0:T(8,128)(2,1)} %reshape.82.refs_0_.refs_1_.refs_2_.refs_3_.refs_4_.refs_5_.refs_6_.refs_7_) | copy-start | bytes 12582916
  16.0 57.8 %copy-start.7 = (s32[8]{0:T(128)S(1)}, s32[8]{0:T(128)}, u32[]{:S(2)}) copy-start(s32[8]{0:T(128)} %param.12) | copy-start | bytes 100
  16.0 58.0 %copy-start.5 = (s32[8,7]{1,0:T(8,128)S(1)}, s32[8,7]{1,0:T(8,128)}, u32[]{:S(2)}) copy-start(s32[8,7]{1,0:T(8,128)} %param.11) | copy-start | bytes 676
  16.0 58.4 %copy-start.6 = (s32[16]{0:T(128)S(1)}, s32[16]{0:T(128)}, u32[]{:S(2)}) copy-start(s32[16]{0:T(128)} %param.13) | copy-start | bytes 196
  16.0 148.7 %copy-start.1 = (bf16[256,1024]{1,0:T(8,128)(2,1)S(1)}, bf16[256,1024]{1,0:T(8,128)(2,1)}, u32[]{:S(2)}) copy-start(bf16[256,1024]{1,0:T(8,128)(2,1)} %constant.52.clone.table_ref) | copy-start | bytes 1572868
  25.6 139.1 %all-gather.7.cloned.1.call-start = ((), (), s32[]{:S(2)}) async-start(), calls=%async_computation.1 | async-start | bytes 18874368 | tf_op jit(solution)/shard_map/all_gather | solution.py:270
Sparse Core Ops, SparseCore 0:
  25.7 48.0 all-gather.4
  75.7 88.9 all-gather.6

commit v2 on v1

--- a/solution.py
+++ b/solution.py
@@ -157,6 +157,127 @@
         compiler_params=pltpu.CompilerParams(vmem_limit_bytes=48 << 20),
     )(*([signal] * RADIX), jnp.asarray(high), jnp.asarray(low), jnp.asarray(near),
       jnp.asarray(count[:, :rows]), jnp.asarray(perm.astype(BF16)))
+
+
+PLANES = 4
+MESH = pl.DeviceIdType.MESH
+
+
+def gather_kernel(own_ref, all_ref, z_send, z_recv, p_send, p_recv, c_send, c_recv, own_sem):
+    chan, seg = lax.axis_index("chan"), lax.axis_index("seg")
+    y, x, core = chan // 4, (chan // 2) % 2, chan % 2
+    x_near = 4 * y + 2 * (1 - x) + core
+    y_near = 4 * (1 - y) + 2 * x + core
+    across = 4 * (1 - y) + 2 * (1 - x) + core
+    twin = 4 * y + 2 * x + (1 - core)
+
+    barrier = pltpu.get_barrier_semaphore()
+    for other in (x_near, y_near, twin):
+        pl.semaphore_signal(barrier, inc=1, device_id=(other, seg), device_id_type=MESH)
+
+    def send(src, dst, send_sem, recv_sem, device):
+        copy = pltpu.make_async_remote_copy(
+            src_ref=src, dst_ref=dst, send_sem=send_sem, recv_sem=recv_sem,
+            device_id=device, device_id_type=MESH,
+        )
+        copy.start()
+        return copy
+
+    def program(z):
+        for step in (1, -1):
+            if 0 <= z + step < PLANES:
+                pl.semaphore_signal(barrier, inc=1, device_id=(chan, z + step), device_id_type=MESH)
+        pl.semaphore_wait(barrier, 3 + (z > 0) + (z < PLANES - 1))
+        sent = []
+        order = sorted(range(PLANES), key=lambda other: abs(other - z))
+        local = pltpu.make_async_copy(own_ref, all_ref.at[chan, z], own_sem)
+        local.start()
+
+        def piece(other):
+            return own_ref if other == z else all_ref.at[chan, other]
+
+        def along(other):
+            for step, side in ((1, 0), (-1, 1)):
+                away = other == z or (z - other) * step > 0
+                if away and 0 <= z + step < PLANES:
+                    sent.append(send(piece(other), all_ref.at[chan, other], z_send.at[other, side],
+                                     z_recv.at[other], (chan, z + step)))
+
+        def landed(ref, sem):
+            pltpu.make_async_remote_copy(
+                src_ref=ref, dst_ref=ref, send_sem=sem, recv_sem=sem,
+                device_id=(twin, z), device_id_type=MESH,
+            ).wait_recv()
+
+        def to_twin(src, block, other, half, slot):
+            sent.append(send(src, all_ref.at[block, other, half], c_send.at[other, slot, half],
+                             c_recv.at[other, slot, half], (twin, z)))
+
+        def outward(other):
+            for half in (0, 1):
+                for way, near in ((0, x_near), (1, y_near)):
+                    part = half if way == 0 else 1 - half
+                    sent.append(send(piece(other).at[part], all_ref.at[chan, other, part],
+                                     p_send.at[other, way, part], p_recv.at[other, way, part], (near, z)))
+            for half in (0, 1):
+                to_twin(piece(other).at[half], chan, other, half, 0)
+
+        def onward(other):
+            for first in (0, 1):
+                for way, block in ((0, x_near), (1, y_near)):
+                    half = first if way == 0 else 1 - first
+                    ref = all_ref.at[block, other, half]
+                    landed(ref, p_recv.at[other, way, half])
+                    if half == way:
+                        sent.append(send(ref, ref, p_send.at[other, 2, half], p_recv.at[other, 2, half],
+                                         ((y_near, x_near)[way], z)))
+                    to_twin(ref, block, other, half, 1 + way)
+
+        def finish(other):
+            for half in (0, 1):
+                ref = all_ref.at[across, other, half]
+                landed(ref, p_recv.at[other, 2, half])
+                to_twin(ref, across, other, half, 3)
+
+        along(z)
+        outward(z)
+        for k in range(1, PLANES):
+            landed(all_ref.at[chan, order[k]], z_recv.at[order[k]])
+            along(order[k])
+            outward(order[k])
+            onward(order[k - 1])
+            if k > 1:
+                finish(order[k - 2])
+        onward(order[-1])
+        finish(order[-2])
+        finish(order[-1])
+        twin_blocks = [4 * y + 2 * x, 4 * y + 2 * (1 - x), 4 * (1 - y) + 2 * x, 4 * (1 - y) + 2 * (1 - x)]
+        for other in range(PLANES):
+            for slot, block in enumerate(twin_blocks):
+                for half in (0, 1):
+                    landed(all_ref.at[block + 1 - core, other, half], c_recv.at[other, slot, half])
+        for copy in sent:
+            copy.wait_send()
+        local.wait()
+
+    for z in range(PLANES):
+        pl.when(seg == z)(functools.partial(program, z))
+
+
+def gather(own):
+    dma = pltpu.SemaphoreType.DMA
+    return pl.pallas_call(
+        gather_kernel,
+        in_specs=[pl.BlockSpec(memory_space=pl.ANY)],
+        out_specs=pl.BlockSpec(memory_space=pl.ANY),
+        out_shape=jax.ShapeDtypeStruct((8, PLANES) + own.shape, own.dtype),
+        scratch_shapes=[
+            dma((PLANES, 2)), dma((PLANES,)),
+            dma((PLANES, 3, 2)), dma((PLANES, 3, 2)),
+            dma((PLANES, 4, 2)), dma((PLANES, 4, 2)), dma,
+        ],
+        compiler_params=pltpu.CompilerParams(collective_id=0, has_side_effects=True),
+    )(own)
 
 
 GROUP = 16
@@ -267,7 +388,10 @@
     norm_factor = 1.0 / math.sqrt(FREQS * local_segs * parts_count)
     signal = traces.reshape(block_size * local_segs, sample_count)
     whitened = whiten(signal, block_size, local_segs)
-    gathered = lax.all_gather(lax.all_gather(whitened, "seg", axis=0), "chan", axis=0)
+    if (block_count, parts_count) == (8, PLANES):
+        gathered = gather(whitened)
+    else:
+        gathered = lax.all_gather(lax.all_gather(whitened, "seg", axis=0), "chan", axis=0)
     slot_first, slot_second = pair_blocks(
         pair_offsets, pair_counts, pair_owner, block_count, pair_owner.shape[0]
     )

time: 201 us -> 129 us (0.64)
  waiting for transfers between devices: 138 us -> 0 us
  Pallas kernels: 38 us -> 115 us
  between operations: 13.5 us -> 0.06 us
    all_gather x2 -> x0, waiting for transfers between devices: 138 us -> none  [the longest x1 89.9 us: on_device(): lax.all_gather(lax.all_gather(whitened, 'seg', axis=0), 'chan', axis=0)]
    pallas_call x0 -> x1, Pallas kernels: none -> 77.4 us  [gather(): pl.pallas_call(gather_kernel, in_specs=[pl.BlockSpec(memory_space=pl.ANY)...]
  transfers between devices with their start and end apart: 2 -> 0, of which waited for: 2 -> 0; matrix products, arithmetic and copies ran while one was open for 0% -> 0% of each run, Pallas kernels for 0% -> 0%
where the time goes in v2:
time: 129 us
  Pallas kernels  115 us (89%)
  local copies, waits for them, and re-layouts  11.2 us (9%)
  other arithmetic  2.65 us (2%)
    pallas_call x1, Pallas kernels, gather(): pl.pallas_call(gather_kernel, in_specs=[pl.BlockSpec(memory_space=pl.ANY)...  77.4 us
    pallas_call x1, Pallas kernels, stack(): pl.pallas_call(functools.partial(stack_kernel, norm_factor, parts, segs,...  28.6 us
    pallas_call x1, Pallas kernels, whiten(): pl.pallas_call(whiten_kernel, grid=(STEPS,), in_specs=[pl.BlockSpec((rows...  8.79 us
    reshape x1, local copies, waits for them, and re-layouts, on_device(): signal = traces.reshape(block_size * local_segs, sample_count)  7.27 us
    unnamed x13, local copies, waits for them, and re-layouts  3.75 us

profile of v2, /device:TPU:1, one launch (start us, length us, event | category | flops | bytes accessed | tf_op | source)
XLA Modules:
  0.0 128.7 jit_solution(12562910644000941606)
XLA Ops:
  0.0 0.8 reduce-window.9
  0.8 0.7 bitcast_subtract_fusion
  1.5 0.1 convert_reduce_fusion
  1.6 0.1 select_reduce_fusion.4
  1.7 0.8 copy.11
  2.5 0.1 select_reduce_fusion
  2.6 0.8 select_reduce_fusion.2
  3.4 0.1 dynamic_slice.6
  3.4 0.1 dynamic_slice.7
  3.5 0.1 pad_add_fusion.index_ref
  3.6 0.0 copy-start.3
  3.6 0.0 copy-start.4
  3.6 0.0 copy-start.5
  3.6 7.3 %reshape.82.refs_0_.refs_1_.refs_2_.refs_3_.refs_4_.refs_5_.refs_6_.refs_7_ = bf16[256,8192]{1,0:T(8,128)(2,1)} reshape(bf16[128,2,8192]{2,1,0:T(2,128)(2,1)} %param.10) | data formatting | bytes 8388608 | tf_op jit(solution)/shard_map/reshape | solution.py:389
  10.9 0.0 copy-done.3
  10.9 0.0 copy-done.4
  10.9 0.0 copy-done.5
  10.9 0.0 copy-start
  10.9 2.2 %copy-done = bf16[256,8192]{1,0:T(8,128)(2,1)S(1)} copy-done((bf16[256,8192]{1,0:T(8,128)(2,1)S(1)}, bf16[256,8192]{1,0:T(8,128)(2,1)}, u32[]{:S(2)}) %copy-start) | copy-done | bytes 4194328
  13.1 8.8 %shard_map.100.own_ref = bf16[2,2,512,128]{3,2,1,0:T(8,128)(2,1)S(1)} custom-call(bf16[256,8192]{1,0:T(8,128)(2,1)S(1)} %copy-done, bf16[256,8192]{1,0:T(8,128)(2,1)S(1)} %copy-done, bf16[256,8192]{1,0:T(8,128)(2,1)S(1)} %copy-done, bf16[256,8192]{1,0:T(8,128)(2,1)S(1)} %copy-done, bf16[256,8192]{1,0:T(8,128)(2,1)S(1)} %copy-done, ...), custom_call_target="tpu_custom_call" | custom-call | tf_op jit(solution)/shard_map/pallas_call | solution.py:147
  21.9 0.0 copy-start.1
  21.9 0.8 copy-done.1
  22.6 0.0 copy-start.2
  22.6 77.4 %shard_map.101.first_ref.second_ref = bf16[8,4,2,2,512,128]{5,4,3,2,1,0:T(8,128)(2,1)} custom-call(bf16[2,2,512,128]{3,2,1,0:T(8,128)(2,1)} %copy-done.1), custom_call_target="tpu_custom_call" | custom-call | tf_op jit(solution)/shard_map/pallas_call | solution.py:269
  100.1 0.0 copy-done.2
  100.1 28.6 %shard_map.102 = f32[32,2,128,256]{3,2,1,0:T(8,128)} custom-call(s32[5]{0:T(128)S(1)} %pad_add_fusion.index_ref, bf16[8,4,2,2,512,128]{5,4,3,2,1,0:T(8,128)(2,1)} %shard_map.101.first_ref.second_ref, bf16[8,4,2,2,512,128]{5,4,3,2,1,0:T(8,128)(2,1)} %shard_map.101.first_ref.second_ref, bf16[256,1024]{1,0:T(8,128)(2,1)S(1)} %copy-done.2), custom_call_target="tpu_custom_call" | custom-call | tf_op jit(solution)/shard_map/pallas_call | solution.py:346
  (5 shorter events, 0.1 us)
Async XLA Ops:
  3.6 7.3 %copy-start.3 = (f32[512,256]{1,0:T(8,128)S(1)}, f32[512,256]{1,0:T(8,128)}, u32[]{:S(2)}) copy-start(f32[512,256]{1,0:T(8,128)} %constant.50.clone.refs_11_) | copy-start | bytes 1572868
  3.6 7.3 %copy-start.4 = (bf16[512,512]{1,0:T(8,128)(2,1)S(1)}, bf16[512,512]{1,0:T(8,128)(2,1)}, u32[]{:S(2)}) copy-start(bf16[512,512]{1,0:T(8,128)(2,1)} %constant.49.clone.refs_10_) | copy-start | bytes 1572868
  3.6 7.3 %copy-start.5 = (bf16[256,256]{1,0:T(8,128)(2,1)S(1)}, bf16[256,256]{1,0:T(8,128)(2,1)}, u32[]{:S(2)}) copy-start(bf16[256,256]{1,0:T(8,128)(2,1)} %constant.51.clone.refs_12_) | copy-start | bytes 393220
  10.9 2.2 %copy-start = (bf16[256,8192]{1,0:T(8,128)(2,1)S(1)}, bf16[256,8192]{1,0:T(8,128)(2,1)}, u32[]{:S(2)}) copy-start(bf16[256,8192]{1,0:T(8,128)(2,1)} %reshape.82.refs_0_.refs_1_.refs_2_.refs_3_.refs_4_.refs_5_.refs_6_.refs_7_) | copy-start | bytes 12582916
  21.9 0.8 copy-start.1
  22.6 77.4 %copy-start.2 = (bf16[256,1024]{1,0:T(8,128)(2,1)S(1)}, bf16[256,1024]{1,0:T(8,128)(2,1)}, u32[]{:S(2)}) copy-start(bf16[256,1024]{1,0:T(8,128)(2,1)} %constant.52.clone.table_ref) | copy-start | bytes 1572868

commit v3 on v2

--- a/solution.py
+++ b/solution.py
@@ -281,9 +281,9 @@
 
 
 GROUP = 16
-FCHUNK = 64
+FCHUNK = 128
 CROSS_STEPS = FREQS // FCHUNK
-ROWS_STEP = 4
+ROWS_STEP = 8
 
 
 def stack_kernel(norm_factor, parts, segs, rows, index_ref, first_ref, second_ref, table_ref, out_ref, cross):

time: 129 us -> 123 us (0.953)
  Pallas kernels: 115 us -> 109 us
    pallas_call x1, Pallas kernels: 28.6 us -> 22.3 us  [stack(): pl.pallas_call(functools.partial(stack_kernel, norm_factor, parts, segs,...]
where the time goes in v3:
time: 123 us; the launch traced here: 122 us
  Pallas kernels  109 us (89%)
  local copies, waits for them, and re-layouts  11.2 us (9%)
  other arithmetic  2.65 us (2%)
    pallas_call x1, Pallas kernels, gather(): pl.pallas_call(gather_kernel, in_specs=[pl.BlockSpec(memory_space=pl.ANY)...  77.4 us
    pallas_call x1, Pallas kernels, stack(): pl.pallas_call(functools.partial(stack_kernel, norm_factor, parts, segs,...  22.3 us
    pallas_call x1, Pallas kernels, whiten(): pl.pallas_call(whiten_kernel, grid=(STEPS,), in_specs=[pl.BlockSpec((rows...  8.79 us
    reshape x1, local copies, waits for them, and re-layouts, on_device(): signal = traces.reshape(block_size * local_segs, sample_count)  7.27 us
    unnamed x13, local copies, waits for them, and re-layouts  3.75 us

profile of v3, /device:TPU:1, one launch (start us, length us, event | category | flops | bytes accessed | tf_op | source)
XLA Modules:
  0.0 122.4 jit_solution(61613784365706831)
XLA Ops:
  0.0 0.8 reduce-window.9
  0.8 0.7 bitcast_subtract_fusion
  1.5 0.1 convert_reduce_fusion
  1.6 0.1 select_reduce_fusion.4
  1.7 0.8 copy.11
  2.5 0.1 select_reduce_fusion
  2.6 0.8 select_reduce_fusion.2
  3.4 0.1 dynamic_slice.6
  3.4 0.1 dynamic_slice.7
  3.5 0.1 pad_add_fusion.index_ref
  3.6 0.0 copy-start.3
  3.6 0.0 copy-start.4
  3.6 0.0 copy-start.5
  3.6 7.3 %reshape.82.refs_0_.refs_1_.refs_2_.refs_3_.refs_4_.refs_5_.refs_6_.refs_7_ = bf16[256,8192]{1,0:T(8,128)(2,1)} reshape(bf16[128,2,8192]{2,1,0:T(2,128)(2,1)} %param.10) | data formatting | bytes 8388608 | tf_op jit(solution)/shard_map/reshape | solution.py:389
  10.9 0.0 copy-done.3
  10.9 0.0 copy-done.4
  10.9 0.0 copy-done.5
  10.9 0.0 copy-start
  10.9 2.2 %copy-done = bf16[256,8192]{1,0:T(8,128)(2,1)S(1)} copy-done((bf16[256,8192]{1,0:T(8,128)(2,1)S(1)}, bf16[256,8192]{1,0:T(8,128)(2,1)}, u32[]{:S(2)}) %copy-start) | copy-done | bytes 4194328
  13.1 8.8 %shard_map.100.own_ref = bf16[2,2,512,128]{3,2,1,0:T(8,128)(2,1)S(1)} custom-call(bf16[256,8192]{1,0:T(8,128)(2,1)S(1)} %copy-done, bf16[256,8192]{1,0:T(8,128)(2,1)S(1)} %copy-done, bf16[256,8192]{1,0:T(8,128)(2,1)S(1)} %copy-done, bf16[256,8192]{1,0:T(8,128)(2,1)S(1)} %copy-done, bf16[256,8192]{1,0:T(8,128)(2,1)S(1)} %copy-done, ...), custom_call_target="tpu_custom_call" | custom-call | tf_op jit(solution)/shard_map/pallas_call | solution.py:147
  21.9 0.0 copy-start.1
  21.9 0.8 copy-done.1
  22.6 0.0 copy-start.2
  22.6 77.4 %shard_map.101.first_ref.second_ref = bf16[8,4,2,2,512,128]{5,4,3,2,1,0:T(8,128)(2,1)} custom-call(bf16[2,2,512,128]{3,2,1,0:T(8,128)(2,1)} %copy-done.1), custom_call_target="tpu_custom_call" | custom-call | tf_op jit(solution)/shard_map/pallas_call | solution.py:269
  100.1 0.0 copy-done.2
  100.1 22.3 %shard_map.102 = f32[32,2,128,256]{3,2,1,0:T(8,128)} custom-call(s32[5]{0:T(128)S(1)} %pad_add_fusion.index_ref, bf16[8,4,2,2,512,128]{5,4,3,2,1,0:T(8,128)(2,1)} %shard_map.101.first_ref.second_ref, bf16[8,4,2,2,512,128]{5,4,3,2,1,0:T(8,128)(2,1)} %shard_map.101.first_ref.second_ref, bf16[256,1024]{1,0:T(8,128)(2,1)S(1)} %copy-done.2), custom_call_target="tpu_custom_call" | custom-call | tf_op jit(solution)/shard_map/pallas_call | solution.py:346
  (5 shorter events, 0.1 us)
Async XLA Ops:
  3.6 7.3 %copy-start.3 = (f32[512,256]{1,0:T(8,128)S(1)}, f32[512,256]{1,0:T(8,128)}, u32[]{:S(2)}) copy-start(f32[512,256]{1,0:T(8,128)} %constant.50.clone.refs_11_) | copy-start | bytes 1572868
  3.6 7.3 %copy-start.4 = (bf16[512,512]{1,0:T(8,128)(2,1)S(1)}, bf16[512,512]{1,0:T(8,128)(2,1)}, u32[]{:S(2)}) copy-start(bf16[512,512]{1,0:T(8,128)(2,1)} %constant.49.clone.refs_10_) | copy-start | bytes 1572868
  3.6 7.3 %copy-start.5 = (bf16[256,256]{1,0:T(8,128)(2,1)S(1)}, bf16[256,256]{1,0:T(8,128)(2,1)}, u32[]{:S(2)}) copy-start(bf16[256,256]{1,0:T(8,128)(2,1)} %constant.51.clone.refs_12_) | copy-start | bytes 393220
  10.9 2.2 %copy-start = (bf16[256,8192]{1,0:T(8,128)(2,1)S(1)}, bf16[256,8192]{1,0:T(8,128)(2,1)}, u32[]{:S(2)}) copy-start(bf16[256,8192]{1,0:T(8,128)(2,1)} %reshape.82.refs_0_.refs_1_.refs_2_.refs_3_.refs_4_.refs_5_.refs_6_.refs_7_) | copy-start | bytes 12582916
  21.9 0.8 copy-start.1
  22.6 77.4 %copy-start.2 = (bf16[256,1024]{1,0:T(8,128)(2,1)S(1)}, bf16[256,1024]{1,0:T(8,128)(2,1)}, u32[]{:S(2)}) copy-start(bf16[256,1024]{1,0:T(8,128)(2,1)} %constant.52.clone.table_ref) | copy-start | bytes 1572868

commit v4 on v1

--- a/solution.py
+++ b/solution.py
@@ -159,10 +159,178 @@
       jnp.asarray(count[:, :rows]), jnp.asarray(perm.astype(BF16)))
 
 
+PLANES = 4
+MESH = pl.DeviceIdType.MESH
+LINE_ROWS = 1536
+
+
+def gather_kernel(own_ref, all_ref, z_send, z_recv, p_send, p_recv, c_send, c_recv,
+                  bz_send, bz_recv, bp_send, bp_recv, bc_send, bc_recv, own_sem):
+    chan, seg = lax.axis_index("chan"), lax.axis_index("seg")
+    y, x, core = chan // 4, (chan // 2) % 2, chan % 2
+    x_near = 4 * y + 2 * (1 - x) + core
+    y_near = 4 * (1 - y) + 2 * x + core
+    across = 4 * (1 - y) + 2 * (1 - x) + core
+    twin = 4 * y + 2 * x + (1 - core)
+    blocks = (chan, x_near, y_near, across)
+    twin_blocks = [block + 1 - 2 * core for block in blocks]
+    near = (x_near, y_near)
+    total_rows = own_ref.shape[0]
+    line = pl.ds(0, LINE_ROWS)
+    line_half = [pl.ds(h * (LINE_ROWS // 2), LINE_ROWS // 2) for h in (0, 1)]
+    rest_rows = total_rows - LINE_ROWS
+    rest = pl.ds(LINE_ROWS, rest_rows)
+    rest_half = [pl.ds(LINE_ROWS + h * (rest_rows // 2), rest_rows // 2) for h in (0, 1)]
+
+    barrier = pltpu.get_barrier_semaphore()
+    for other in (x_near, y_near, twin):
+        pl.semaphore_signal(barrier, inc=1, device_id=(other, seg), device_id_type=MESH)
+
+    def program(z):
+        for step in (1, -1):
+            if 0 <= z + step < PLANES:
+                pl.semaphore_signal(barrier, inc=1, device_id=(chan, z + step), device_id_type=MESH)
+        pl.semaphore_wait(barrier, 3 + int(z > 0) + int(z < PLANES - 1))
+        sent = []
+        order = sorted(range(PLANES), key=lambda other: abs(other - z))
+
+        def send(src, dst, send_sem, recv_sem, device):
+            copy = pltpu.make_async_remote_copy(
+                src_ref=src, dst_ref=dst, send_sem=send_sem, recv_sem=recv_sem,
+                device_id=device, device_id_type=MESH,
+            )
+            copy.start()
+            sent.append(copy)
+
+        def landed(ref, sem):
+            pltpu.make_async_remote_copy(
+                src_ref=ref, dst_ref=ref, send_sem=sem, recv_sem=sem,
+                device_id=(twin, z), device_id_type=MESH,
+            ).wait_recv()
+
+        def part(block, other, rows):
+            if block == 0 and other == z:
+                return own_ref.at[rows]
+            return all_ref.at[blocks[block], other, rows]
+
+        def along(block, other, rows, send_sem, recv_sem):
+            for step, side in ((1, 0), (-1, 1)):
+                away = other == z or (z - other) * step > 0
+                if away and 0 <= z + step < PLANES:
+                    send(part(block, other, rows), all_ref.at[blocks[block], other, rows],
+                         send_sem.at[other, block, side], recv_sem.at[other, block], (chan, z + step))
+
+        def to_twin(block, other, rows, send_sem, recv_sem, half):
+            send(part(block, other, rows), all_ref.at[blocks[block], other, rows],
+                 send_sem.at[other, block, half], recv_sem.at[other, block, half], (twin, z))
+
+        def outward(other, halves, send_sem, recv_sem):
+            for first in (0, 1):
+                for way in (0, 1):
+                    half = first if way == 0 else 1 - first
+                    send(part(0, other, halves[half]), all_ref.at[chan, other, halves[half]],
+                         send_sem.at[other, way, half], recv_sem.at[other, way, half], (near[way], z))
+
+        def onward(other, halves, send_sem, recv_sem, first):
+            for way in (0, 1):
+                half = first if way == 0 else 1 - first
+                ref = all_ref.at[near[way], other, halves[half]]
+                landed(ref, recv_sem.at[other, way, half])
+                if half == way:
+                    send(ref, ref, send_sem.at[other, 2, half], recv_sem.at[other, 2, half],
+                         (near[1 - way], z))
+
+        def finish(other, halves, recv_sem):
+            for half in (0, 1):
+                landed(all_ref.at[across, other, halves[half]], recv_sem.at[other, 2, half])
+
+        def line_out(other):
+            outward(other, line_half, p_send, p_recv)
+            for half in (0, 1):
+                to_twin(0, other, line_half[half], c_send, c_recv, half)
+
+        def line_on(other):
+            for first in (0, 1):
+                onward(other, line_half, p_send, p_recv, first)
+                to_twin(1, other, line_half[first], c_send, c_recv, first)
+                to_twin(2, other, line_half[1 - first], c_send, c_recv, 1 - first)
+
+        def line_finish(other):
+            finish(other, line_half, p_recv)
+            for half in (0, 1):
+                to_twin(3, other, line_half[half], c_send, c_recv, half)
+
+        def rest_line(other):
+            for block in range(4):
+                landed(all_ref.at[blocks[block], other, rest], bz_recv.at[other, block])
+                along(block, other, rest, bz_send, bz_recv)
+                to_twin(block, other, rest, bc_send, bc_recv, 0)
+
+        along(0, z, line, z_send, z_recv)
+        outward(z, rest_half, bp_send, bp_recv)
+        along(0, z, rest, bz_send, bz_recv)
+        to_twin(0, z, rest, bc_send, bc_recv, 0)
+        local = pltpu.make_async_copy(own_ref, all_ref.at[chan, z], own_sem)
+        local.start()
+        line_out(z)
+        for first in (0, 1):
+            onward(z, rest_half, bp_send, bp_recv, first)
+        for block in (1, 2):
+            along(block, z, rest, bz_send, bz_recv)
+            to_twin(block, z, rest, bc_send, bc_recv, 0)
+        finish(z, rest_half, bp_recv)
+        along(3, z, rest, bz_send, bz_recv)
+        to_twin(3, z, rest, bc_send, bc_recv, 0)
+        for k in range(1, PLANES):
+            landed(all_ref.at[chan, order[k], line], z_recv.at[order[k], 0])
+            along(0, order[k], line, z_send, z_recv)
+            line_out(order[k])
+            line_on(order[k - 1])
+            rest_line(order[k])
+            if k > 1:
+                line_finish(order[k - 2])
+        line_on(order[-1])
+        line_finish(order[-2])
+        line_finish(order[-1])
+        for other in range(PLANES):
+            for block in range(4):
+                ref = all_ref.at[twin_blocks[block], other]
+                for half in (0, 1):
+                    landed(ref.at[line_half[half]], c_recv.at[other, block, half])
+                landed(ref.at[rest], bc_recv.at[other, block, 0])
+        for copy in sent:
+            copy.wait_send()
+        local.wait()
+
+    for z in range(PLANES):
+        pl.when(seg == z)(functools.partial(program, z))
+
+
+def gather(own):
+    dma = pltpu.SemaphoreType.DMA
+    rows, lanes = math.prod(own.shape[:-1]), own.shape[-1]
+    gathered = pl.pallas_call(
+        gather_kernel,
+        in_specs=[pl.BlockSpec(memory_space=pl.ANY)],
+        out_specs=pl.BlockSpec(memory_space=pl.ANY),
+        out_shape=jax.ShapeDtypeStruct((8, PLANES, rows, lanes), own.dtype),
+        scratch_shapes=[
+            dma((PLANES, 1, 2)), dma((PLANES, 1)),
+            dma((PLANES, 3, 2)), dma((PLANES, 3, 2)),
+            dma((PLANES, 4, 2)), dma((PLANES, 4, 2)),
+            dma((PLANES, 4, 2)), dma((PLANES, 4)),
+            dma((PLANES, 3, 2)), dma((PLANES, 3, 2)),
+            dma((PLANES, 4, 1)), dma((PLANES, 4, 1)), dma,
+        ],
+        compiler_params=pltpu.CompilerParams(collective_id=0, has_side_effects=True),
+    )(own.reshape(rows, lanes))
+    return gathered.reshape((8, PLANES) + own.shape)
+
+
 GROUP = 16
-FCHUNK = 64
+FCHUNK = 128
 CROSS_STEPS = FREQS // FCHUNK
-ROWS_STEP = 4
+ROWS_STEP = 8
 
 
 def stack_kernel(norm_factor, parts, segs, rows, index_ref, first_ref, second_ref, table_ref, out_ref, cross):
@@ -267,7 +435,10 @@
     norm_factor = 1.0 / math.sqrt(FREQS * local_segs * parts_count)
     signal = traces.reshape(block_size * local_segs, sample_count)
     whitened = whiten(signal, block_size, local_segs)
-    gathered = lax.all_gather(lax.all_gather(whitened, "seg", axis=0), "chan", axis=0)
+    if (block_count, parts_count) == (8, PLANES):
+        gathered = gather(whitened)
+    else:
+        gathered = lax.all_gather(lax.all_gather(whitened, "seg", axis=0), "chan", axis=0)
     slot_first, slot_second = pair_blocks(
         pair_offsets, pair_counts, pair_owner, block_count, pair_owner.shape[0]
     )

time: 201 us -> 121 us (0.60)
  waiting for transfers between devices: 138 us -> 0 us
  Pallas kernels: 38 us -> 107 us
  between operations: 13.5 us -> 0.06 us
    all_gather x2 -> x0, waiting for transfers between devices: 138 us -> none  [the longest x1 89.9 us: on_device(): lax.all_gather(lax.all_gather(whitened, 'seg', axis=0), 'chan', axis=0)]
    pallas_call x0 -> x1, Pallas kernels: none -> 75.6 us  [gather(): pl.pallas_call(gather_kernel, in_specs=[pl.BlockSpec(memory_space=pl.ANY)...]
    pallas_call x1, Pallas kernels: 28.5 us -> 22.3 us  [stack(): pl.pallas_call(functools.partial(stack_kernel, norm_factor, parts, segs,...]
  transfers between devices with their start and end apart: 2 -> 0, of which waited for: 2 -> 0; matrix products, arithmetic and copies ran while one was open for 0% -> 0% of each run, Pallas kernels for 0% -> 0%
where the time goes in v4:
time: 121 us
  Pallas kernels  107 us (88%)
  local copies, waits for them, and re-layouts  11.2 us (9%)
  other arithmetic  2.65 us (2%)
    pallas_call x1, Pallas kernels, gather(): pl.pallas_call(gather_kernel, in_specs=[pl.BlockSpec(memory_space=pl.ANY)...  75.6 us
    pallas_call x1, Pallas kernels, stack(): pl.pallas_call(functools.partial(stack_kernel, norm_factor, parts, segs,...  22.3 us
    pallas_call x1, Pallas kernels, whiten(): pl.pallas_call(whiten_kernel, grid=(STEPS,), in_specs=[pl.BlockSpec((rows...  8.79 us
    reshape x1, local copies, waits for them, and re-layouts, on_device(): signal = traces.reshape(block_size * local_segs, sample_count)  7.27 us
    unnamed x13, local copies, waits for them, and re-layouts  3.75 us

profile of v4, /device:TPU:1, one launch (start us, length us, event | category | flops | bytes accessed | tf_op | source)
XLA Modules:
  0.0 120.5 jit_solution(7926993607048682082)
XLA Ops:
  0.0 0.8 reduce-window.9
  0.8 0.7 bitcast_subtract_fusion
  1.5 0.1 convert_reduce_fusion
  1.6 0.1 select_reduce_fusion.4
  1.7 0.8 copy.11
  2.5 0.1 select_reduce_fusion
  2.6 0.8 select_reduce_fusion.2
  3.4 0.1 dynamic_slice.6
  3.4 0.1 dynamic_slice.7
  3.5 0.1 pad_add_fusion.index_ref
  3.6 0.0 copy-start.3
  3.6 0.0 copy-start.4
  3.6 0.0 copy-start.5
  3.6 7.3 %reshape.88.refs_0_.refs_1_.refs_2_.refs_3_.refs_4_.refs_5_.refs_6_.refs_7_ = bf16[256,8192]{1,0:T(8,128)(2,1)} reshape(bf16[128,2,8192]{2,1,0:T(2,128)(2,1)} %param.10) | data formatting | bytes 8388608 | tf_op jit(solution)/shard_map/reshape | solution.py:436
  10.9 0.0 copy-done.3
  10.9 0.0 copy-done.4
  10.9 0.0 copy-done.5
  10.9 0.0 copy-start
  10.9 2.2 %copy-done = bf16[256,8192]{1,0:T(8,128)(2,1)S(1)} copy-done((bf16[256,8192]{1,0:T(8,128)(2,1)S(1)}, bf16[256,8192]{1,0:T(8,128)(2,1)}, u32[]{:S(2)}) %copy-start) | copy-done | bytes 4194328
  13.1 8.8 %shard_map.100 = bf16[2,2,512,128]{3,2,1,0:T(8,128)(2,1)S(1)} custom-call(bf16[256,8192]{1,0:T(8,128)(2,1)S(1)} %copy-done, bf16[256,8192]{1,0:T(8,128)(2,1)S(1)} %copy-done, bf16[256,8192]{1,0:T(8,128)(2,1)S(1)} %copy-done, bf16[256,8192]{1,0:T(8,128)(2,1)S(1)} %copy-done, bf16[256,8192]{1,0:T(8,128)(2,1)S(1)} %copy-done, bf16[256,8192]{1,0:T(8,128)(2,1)S(1)} %copy-done, ...), custom_call_target="tpu_custom_call" | custom-call | tf_op jit(solution)/shard_map/pallas_call | solution.py:147
  21.9 0.0 copy-start.1
  21.9 0.8 copy-done.1
  22.6 0.0 copy-start.2
  22.6 75.6 %shard_map.101 = bf16[8,4,2048,128]{3,2,1,0:T(8,128)(2,1)} custom-call(bf16[2048,128]{1,0:T(8,128)(2,1)} %bitcast.6), custom_call_target="tpu_custom_call" | custom-call | tf_op jit(solution)/shard_map/pallas_call | solution.py:312
  98.2 0.0 copy-done.2
  98.2 22.3 %shard_map.102 = f32[32,2,128,256]{3,2,1,0:T(8,128)} custom-call(s32[5]{0:T(128)S(1)} %pad_add_fusion.index_ref, bf16[8,4,2,2,512,128]{5,4,3,2,1,0:T(8,128)(2,1)} %bitcast.7, bf16[8,4,2,2,512,128]{5,4,3,2,1,0:T(8,128)(2,1)} %bitcast.8, bf16[256,1024]{1,0:T(8,128)(2,1)S(1)} %copy-done.2), custom_call_target="tpu_custom_call" | custom-call | tf_op jit(solution)/shard_map/pallas_call | solution.py:393
  (5 shorter events, 0.1 us)
Async XLA Ops:
  3.6 7.3 %copy-start.3 = (f32[512,256]{1,0:T(8,128)S(1)}, f32[512,256]{1,0:T(8,128)}, u32[]{:S(2)}) copy-start(f32[512,256]{1,0:T(8,128)} %constant.50.clone.refs_11_) | copy-start | bytes 1572868
  3.6 7.3 %copy-start.4 = (bf16[512,512]{1,0:T(8,128)(2,1)S(1)}, bf16[512,512]{1,0:T(8,128)(2,1)}, u32[]{:S(2)}) copy-start(bf16[512,512]{1,0:T(8,128)(2,1)} %constant.49.clone.refs_10_) | copy-start | bytes 1572868
  3.6 7.3 %copy-start.5 = (bf16[256,256]{1,0:T(8,128)(2,1)S(1)}, bf16[256,256]{1,0:T(8,128)(2,1)}, u32[]{:S(2)}) copy-start(bf16[256,256]{1,0:T(8,128)(2,1)} %constant.51.clone.refs_12_) | copy-start | bytes 393220
  10.9 2.2 %copy-start = (bf16[256,8192]{1,0:T(8,128)(2,1)S(1)}, bf16[256,8192]{1,0:T(8,128)(2,1)}, u32[]{:S(2)}) copy-start(bf16[256,8192]{1,0:T(8,128)(2,1)} %reshape.88.refs_0_.refs_1_.refs_2_.refs_3_.refs_4_.refs_5_.refs_6_.refs_7_) | copy-start | bytes 12582916
  21.9 0.8 copy-start.1
  22.6 75.6 %copy-start.2 = (bf16[256,1024]{1,0:T(8,128)(2,1)S(1)}, bf16[256,1024]{1,0:T(8,128)(2,1)}, u32[]{:S(2)}) copy-start(bf16[256,1024]{1,0:T(8,128)(2,1)} %constant.52.clone.table_ref) | copy-start | bytes 1572868

commit v5 on v4

--- a/solution.py
+++ b/solution.py
@@ -21,8 +21,8 @@
 FOLDED = SAMPLES // RADIX
 RESIDUES = (0, 4, 1, 7, 2, 6, 3, 5)
 PER_RES = FREQS // RADIX
-CHUNK = 256
-STEPS = FOLDED // CHUNK
+LANES = 128
+PARTS = FOLDED // LANES
 BF16 = ml_dtypes.bfloat16
 
 BIN_ORDER = np.concatenate([np.arange(PER_RES) * RADIX + r for r in RESIDUES])
@@ -47,8 +47,7 @@
         for i, (a, b) in enumerate(rows):
             full[group, i * PER_RES:(i + 1) * PER_RES, 0] = a
             full[group, i * PER_RES:(i + 1) * PER_RES, 1] = b
-    full = full.reshape(4, 4 * PER_RES, 2, STEPS, CHUNK).transpose(3, 0, 1, 2, 4)
-    full = full.reshape(STEPS, 4, 4 * PER_RES, 2 * CHUNK).astype(np.float32)
+    full = full.reshape(4, 4 * PER_RES, 2 * FOLDED).astype(np.float32)
     high = full.astype(BF16)
     low = (full - high.astype(np.float32)).astype(BF16)
     return high, low
@@ -60,10 +59,8 @@
     return np.concatenate([np.cos(angle), -np.sin(angle)], axis=1).astype(np.float32).astype(BF16)
 
 
-def window_tables():
-    near = np.abs(BIN_ORDER[:, None] - BIN_ORDER[None, :]) <= HALF
-    count = near.sum(axis=1).astype(np.float32)
-    return near.astype(BF16), np.ascontiguousarray(np.broadcast_to(count[:, None], (FREQS, 256)))
+def window_table():
+    return (np.abs(BIN_ORDER[:, None] - BIN_ORDER[None, :]) <= HALF).astype(BF16)
 
 
 def split(value):
@@ -79,89 +76,135 @@
     return jnp.dot(a, b, preferred_element_type=jnp.float32)
 
 
-def whiten_kernel(*refs):
-    xs = refs[:RADIX]
-    high_ref, low_ref, near_ref, count_ref, perm_ref, out_ref, total = refs[RADIX:]
+def list_pairs(offsets_ref, counts_ref, owner_ref, index_ref):
+    blocks = counts_ref.shape[0]
+    my_start = lax.axis_index("chan") * TILE_DEV
+    for i in range(2 * TILE_DEV):
+        index_ref[i] = 0
+    index_ref[2 * TILE_DEV] = lax.axis_index("seg")
+
+    def one_block(a, start):
+        def one_pair(rank, carry):
+            slot = owner_ref[start + rank] - my_start
+
+            @pl.when((slot >= 0) & (slot < TILE_DEV))
+            def _():
+                index_ref[slot] = a
+                index_ref[TILE_DEV + slot] = lax.rem(a + offsets_ref[a, rank], blocks)
+
+            return carry
+
+        lax.fori_loop(0, counts_ref[a], one_pair, 0)
+        return start + counts_ref[a]
+
+    lax.fori_loop(0, blocks, one_block, 0)
+
+
+def whiten_kernel(x_ref, high_ref, low_ref, near_ref, offsets_ref, counts_ref, owner_ref,
+                  out_ref, index_ref, folded, total):
     step = pl.program_id(0)
+    block_size = x_ref.shape[0]
+    segs = out_ref.shape[0]
+    deep = PARTS * segs
+    some = 2
 
     @pl.when(step == 0)
     def _():
-        total[...] = jnp.zeros_like(total)
-
-    x = [ref[...].astype(jnp.float32) for ref in xs]
-    e0, e1, e2, e3 = x[0] + x[4], x[1] + x[5], x[2] + x[6], x[3] + x[7]
-    d0, d1, d2, d3 = x[0] - x[4], x[1] - x[5], x[2] - x[6], x[3] - x[7]
-    root = math.sqrt(0.5)
-    plus, minus = (d1 + d3) * root, (d1 - d3) * root
-    folded = (
-        ((e0 + e2) + (e1 + e3), (e0 + e2) - (e1 + e3)),
-        (d0 + minus, -(d2 + plus)),
-        (e0 - e2, e3 - e1),
-        (d0 - minus, d2 - plus),
-    )
-    for group, (a, b) in enumerate(folded):
-        a_high, a_low = split(a)
-        b_high, b_low = split(b)
-        y_high = jnp.concatenate([a_high, b_high], axis=1)
-        y_low = jnp.concatenate([a_low, b_low], axis=1)
-        t_high = high_ref[0, group]
-        part = dot_nt(t_high, y_high) + dot_nt(t_high, y_low) + dot_nt(low_ref[0, group], y_high)
-        total[group] += part
-
-    @pl.when(step == STEPS - 1)
+        list_pairs(offsets_ref, counts_ref, owner_ref, index_ref)
+
+        def fold(i, carry):
+            at = i * some
+            x = [
+                x_ref[pl.ds(at, some), j * deep:(j + 1) * deep, :].astype(jnp.float32)
+                for j in range(RADIX)
+            ]
+            e0, e1, e2, e3 = x[0] + x[4], x[1] + x[5], x[2] + x[6], x[3] + x[7]
+            d0, d1, d2, d3 = x[0] - x[4], x[1] - x[5], x[2] - x[6], x[3] - x[7]
+            root = math.sqrt(0.5)
+            plus, minus = (d1 + d3) * root, (d1 - d3) * root
+            values = (
+                (e0 + e2) + (e1 + e3), (e0 + e2) - (e1 + e3),
+                d0 + minus, -(d2 + plus),
+                e0 - e2, e3 - e1,
+                d0 - minus, d2 - plus,
+            )
+            for j, value in enumerate(values):
+                rows = pl.ds(pl.multiple_of(at * deep, some * deep), some * deep)
+                folded[j // 2, j % 2, rows, :] = value.reshape(some * deep, LANES)
+            return carry
+
+        lax.fori_loop(0, block_size // some, fold, 0, unroll=2)
+
+    pieces = []
+    for half in range(2):
+        for part in range(PARTS):
+            column = [
+                folded[step, half, pl.ds(part * segs + s, block_size, stride=deep), :]
+                for s in range(segs)
+            ]
+            pieces.append(split(jnp.concatenate(column, axis=0)))
+    y_high = jnp.concatenate([piece[0] for piece in pieces], axis=1)
+    y_low = jnp.concatenate([piece[1] for piece in pieces], axis=1)
+    t_high = high_ref[0]
+    total[step] = dot_nt(t_high, y_high) + dot_nt(t_high, y_low) + dot_nt(low_ref[0], y_high)
+
+    @pl.when(step == pl.num_programs(0) - 1)
     def _():
-        real, imag = [], []
+        real, imag, counts = [], [], []
+        width = segs * block_size
         for group in range(4):
             for half in range(2):
                 base = half * 2 * PER_RES
                 real.append(total[group, base:base + PER_RES])
                 imag.append(total[group, base + PER_RES:base + 2 * PER_RES])
+                bins = lax.broadcasted_iota(jnp.int32, (PER_RES, width), 0) * RADIX
+                bins = bins + RESIDUES[2 * group + half]
+                ends = jnp.minimum(bins + HALF, FREQS - 1) - jnp.maximum(bins - HALF, 0)
+                counts.append((ends + 1).astype(jnp.float32))
         real = jnp.concatenate(real, axis=0)
         imag = jnp.concatenate(imag, axis=0)
         amplitude = jnp.sqrt(real * real + imag * imag)
-        high, rest = amplitude.astype(jnp.bfloat16), None
-        rest = amplitude - high.astype(jnp.float32)
-        mid, low = split(rest)
+        high = amplitude.astype(jnp.bfloat16)
+        mid, low = split(amplitude - high.astype(jnp.float32))
         near = near_ref[...]
         summed = dot_nn(near, high) + (dot_nn(near, mid) + dot_nn(near, low))
-        divisor = jnp.maximum(summed / count_ref[...], 1.0)
-        segs = out_ref.shape[0]
+        divisor = jnp.maximum(summed / jnp.concatenate(counts, axis=0), 1.0)
         for part, value in enumerate((real, imag)):
             white = (value / divisor).astype(jnp.bfloat16)
-            moved = dot_nn(white, perm_ref[...]).astype(jnp.bfloat16)
-            width = moved.shape[1] // segs
             for s in range(segs):
-                out_ref[s, part] = moved[:, s * width:(s + 1) * width]
-
-
-def whiten(signal, block_size, segs):
-    rows = block_size * segs
+                out_ref[s, part] = white[:, s * block_size:(s + 1) * block_size]
+
+
+def whiten(traces, pair_offsets, pair_counts, pair_owner):
+    block_size, segs, samples = traces.shape
+    pieces = samples // LANES
+    laid = traces.reshape(block_size, segs, pieces, LANES).transpose(0, 2, 1, 3)
+    laid = laid.reshape(block_size, pieces * segs, LANES)
     high, low = dft_tables()
-    near, count = window_tables()
-    perm = np.zeros((rows, rows), np.float32)
-    for c in range(block_size):
-        for s in range(segs):
-            perm[c * segs + s, s * block_size + c] = 1.0
-    once = lambda shape: pl.BlockSpec(shape, lambda q: (0,) * len(shape))
-    table = pl.BlockSpec((1, 4, 4 * PER_RES, 2 * CHUNK), lambda q: (q, 0, 0, 0))
+    once = lambda shape: pl.BlockSpec(shape, lambda g: (0,) * len(shape))
+    table = pl.BlockSpec((1, 4 * PER_RES, 2 * FOLDED), lambda g: (g, 0, 0))
+    scalars = pl.BlockSpec(memory_space=pltpu.SMEM)
     return pl.pallas_call(
         whiten_kernel,
-        grid=(STEPS,),
-        in_specs=[
-            pl.BlockSpec((rows, CHUNK), functools.partial(lambda j, q: (0, j * STEPS + q), j))
-            for j in range(RADIX)
-        ] + [table, table, once((FREQS, FREQS)), once((FREQS, 256)), once((rows, rows))],
-        out_specs=once((segs, 2, FREQS, block_size)),
-        out_shape=jax.ShapeDtypeStruct((segs, 2, FREQS, block_size), jnp.bfloat16),
-        scratch_shapes=[pltpu.VMEM((4, 4 * PER_RES, rows), jnp.float32)],
-        compiler_params=pltpu.CompilerParams(vmem_limit_bytes=48 << 20),
-    )(*([signal] * RADIX), jnp.asarray(high), jnp.asarray(low), jnp.asarray(near),
-      jnp.asarray(count[:, :rows]), jnp.asarray(perm.astype(BF16)))
+        grid=(4,),
+        in_specs=[once(laid.shape), table, table, once((FREQS, FREQS)), scalars, scalars, scalars],
+        out_specs=[once((segs, 2, FREQS, block_size)), scalars],
+        out_shape=[
+            jax.ShapeDtypeStruct((segs, 2, FREQS, block_size), jnp.bfloat16),
+            jax.ShapeDtypeStruct((8,), jnp.int32),
+        ],
+        scratch_shapes=[
+            pltpu.VMEM((4, 2, block_size * PARTS * segs, LANES), jnp.float32),
+            pltpu.VMEM((4, 4 * PER_RES, block_size * segs), jnp.float32),
+        ],
+        compiler_params=pltpu.CompilerParams(vmem_limit_bytes=56 << 20),
+    )(laid, jnp.asarray(high), jnp.asarray(low), jnp.asarray(window_table()),
+      pair_offsets, pair_counts, pair_owner)
 
 
 PLANES = 4
 MESH = pl.DeviceIdType.MESH
-LINE_ROWS = 1536
+LINE_ROWS = 1792
 
 
 def gather_kernel(own_ref, all_ref, z_send, z_recv, p_send, p_recv, c_send, c_recv,
@@ -411,45 +454,16 @@
     )(index, gathered, gathered, jnp.asarray(lag_table()))
 
 
-def pair_blocks(pair_offsets, pair_counts, pair_owner, block_count, slot_count):
-    slot_index = lax.iota(jnp.int32, slot_count)
-    starts = jnp.cumsum(pair_counts) - pair_counts
-    first_block = jnp.sum((starts[None, :] <= slot_index[:, None]).astype(jnp.int32), axis=1) - 1
-    member = lax.iota(jnp.int32, block_count)[None, :] == first_block[:, None]
-    start_of = jnp.sum(jnp.where(member, starts[None, :], 0), axis=1)
-    position = slot_index - start_of
-    listed = jnp.sum(jnp.where(member[:, :, None], pair_offsets[None, :, :], 0), axis=1)
-    chosen = lax.iota(jnp.int32, pair_offsets.shape[1])[None, :] == position[:, None]
-    offset = jnp.sum(jnp.where(chosen, listed, 0), axis=1)
-    second_block = jnp.mod(first_block + offset, block_count)
-    held = pair_owner[None, :] == slot_index[:, None]
-    slot_first = jnp.sum(jnp.where(held, first_block[None, :], 0), axis=1)
-    slot_second = jnp.sum(jnp.where(held, second_block[None, :], 0), axis=1)
-    return (slot_first, slot_second)
-
-
 def on_device(traces, pair_offsets, pair_counts, pair_owner):
     block_size, local_segs, sample_count = traces.shape
     parts_count = lax.axis_size("seg")
     block_count = lax.axis_size("chan")
     norm_factor = 1.0 / math.sqrt(FREQS * local_segs * parts_count)
-    signal = traces.reshape(block_size * local_segs, sample_count)
-    whitened = whiten(signal, block_size, local_segs)
+    whitened, index = whiten(traces, pair_offsets, pair_counts, pair_owner)
     if (block_count, parts_count) == (8, PLANES):
         gathered = gather(whitened)
     else:
         gathered = lax.all_gather(lax.all_gather(whitened, "seg", axis=0), "chan", axis=0)
-    slot_first, slot_second = pair_blocks(
-        pair_offsets, pair_counts, pair_owner, block_count, pair_owner.shape[0]
-    )
-    my_start = lax.axis_index("chan") * TILE_DEV
-    index = jnp.concatenate(
-        [
-            lax.dynamic_slice_in_dim(slot_first, my_start, TILE_DEV),
-            lax.dynamic_slice_in_dim(slot_second, my_start, TILE_DEV),
-            lax.axis_index("seg")[None],
-        ]
-    ).astype(jnp.int32)
     return stack(index, gathered, norm_factor, block_size // parts_count)
 
 

time: 121 us -> 107 us (0.88)
  local copies, waits for them, and re-layouts: 11.2 us -> 0.01 us
  other arithmetic: 2.65 us -> 0 us
    reshape x1 -> x0, local copies, waits for them, and re-layouts: 7.27 us -> none  [on_device(): signal = traces.reshape(block_size * local_segs, sample_count)]
    unnamed x13 -> x4, local copies, waits for them, and re-layouts: 3.75 us -> 0.01 us
    pallas_call x1, Pallas kernels: 8.79 us -> 12.2 us  [whiten(): pl.pallas_call(whiten_kernel, grid=(4,), in_specs=[once(laid.shape), tabl...]
    pallas_call x1, Pallas kernels: 75.6 us -> 72.2 us  [gather(): pl.pallas_call(gather_kernel, in_specs=[pl.BlockSpec(memory_space=pl.ANY)...]
where the time goes in v5:
time: 107 us
  Pallas kernels  107 us (100%)
    pallas_call x1, Pallas kernels, gather(): pl.pallas_call(gather_kernel, in_specs=[pl.BlockSpec(memory_space=pl.ANY)...  72.2 us
    pallas_call x1, Pallas kernels, stack(): pl.pallas_call(functools.partial(stack_kernel, norm_factor, parts, segs,...  22.3 us
    pallas_call x1, Pallas kernels, whiten(): pl.pallas_call(whiten_kernel, grid=(4,), in_specs=[once(laid.shape), tabl...  12.2 us

profile of v5, /device:TPU:1, one launch (start us, length us, event | category | flops | bytes accessed | tf_op | source)
XLA Modules:
  0.0 106.7 jit_solution(11732832018746618664)
XLA Ops:
  0.0 12.2 %shard_map.82 = (bf16[2,2,512,128]{3,2,1,0:T(8,128)(2,1)}, s32[8]{0:T(128)}) custom-call(bf16[128,128,128]{2,1,0:T(8,128)(2,1)} %bitcast.9, bf16[4,256,2048]{2,1,0:T(8,128)(2,1)} %constant.8.clone.high_ref, bf16[4,256,2048]{2,1,0:T(8,128)(2,1)} %constant.9.clone.low_ref, bf16[512,512]{1,0:T(8,128)(2,1)} %constant.10.clone.near_ref, s32[8,7]{1,0:T(8,128)} %offsets_ref.1, ...), custom_call_target="tpu_custom_call" | custom-call | tf_op jit(solution)/shard_map/pallas_call | solution.py:187
  12.2 0.0 copy-start
  12.2 0.0 copy-start.1
  12.2 72.2 %shard_map.83 = bf16[8,4,2048,128]{3,2,1,0:T(8,128)(2,1)} custom-call(bf16[2048,128]{1,0:T(8,128)(2,1)} %bitcast.10), custom_call_target="tpu_custom_call" | custom-call | tf_op jit(solution)/shard_map/pallas_call | solution.py:355
  84.4 0.0 copy-done
  84.4 0.0 copy-done.1
  84.4 22.3 %shard_map.84 = f32[32,2,128,256]{3,2,1,0:T(8,128)} custom-call(s32[8]{0:T(128)S(1)} %copy-done.1, bf16[8,4,2,2,512,128]{5,4,3,2,1,0:T(8,128)(2,1)} %bitcast.7, bf16[8,4,2,2,512,128]{5,4,3,2,1,0:T(8,128)(2,1)} %bitcast.8, bf16[256,1024]{1,0:T(8,128)(2,1)S(1)} %copy-done), custom_call_target="tpu_custom_call" | custom-call | tf_op jit(solution)/shard_map/pallas_call | solution.py:436
Async XLA Ops:
  12.2 72.2 %copy-start = (bf16[256,1024]{1,0:T(8,128)(2,1)S(1)}, bf16[256,1024]{1,0:T(8,128)(2,1)}, u32[]{:S(2)}) copy-start(bf16[256,1024]{1,0:T(8,128)(2,1)} %constant.11.clone.table_ref) | copy-start | bytes 1572868
  12.2 72.2 %copy-start.1 = (s32[8]{0:T(128)S(1)}, s32[8]{0:T(128)}, u32[]{:S(2)}) copy-start(s32[8]{0:T(128)} %get-tuple-element.7.index_ref) | copy-start | bytes 100

commit v6 on v5

--- a/solution.py
+++ b/solution.py
@@ -204,7 +204,7 @@
 
 PLANES = 4
 MESH = pl.DeviceIdType.MESH
-LINE_ROWS = 1792
+LINE_ROWS = 1664
 
 
 def gather_kernel(own_ref, all_ref, z_send, z_recv, p_send, p_recv, c_send, c_recv,
@@ -371,9 +371,9 @@
 
 
 GROUP = 16
-FCHUNK = 128
+FCHUNK = 256
 CROSS_STEPS = FREQS // FCHUNK
-ROWS_STEP = 8
+ROWS_STEP = 16
 
 
 def stack_kernel(norm_factor, parts, segs, rows, index_ref, first_ref, second_ref, table_ref, out_ref, cross):

time: 107 us -> 107 us (level)
    pallas_call x1, Pallas kernels: 22.3 us -> 20.7 us  [stack(): pl.pallas_call(functools.partial(stack_kernel, norm_factor, parts, segs,...]
    pallas_call x1, Pallas kernels: 72.2 us -> 73.5 us  [gather(): pl.pallas_call(gather_kernel, in_specs=[pl.BlockSpec(memory_space=pl.ANY)...]
where the time goes in v6:
time: 107 us; the launch traced here: 106 us
  Pallas kernels  106 us (99%)
    pallas_call x1, Pallas kernels, gather(): pl.pallas_call(gather_kernel, in_specs=[pl.BlockSpec(memory_space=pl.ANY)...  73.5 us
    pallas_call x1, Pallas kernels, stack(): pl.pallas_call(functools.partial(stack_kernel, norm_factor, parts, segs,...  20.7 us
    pallas_call x1, Pallas kernels, whiten(): pl.pallas_call(whiten_kernel, grid=(4,), in_specs=[once(laid.shape), tabl...  12.2 us

profile of v6, /device:TPU:1, one launch (start us, length us, event | category | flops | bytes accessed | tf_op | source)
XLA Modules:
  0.0 106.4 jit_solution(5962554680809531003)
XLA Ops:
  0.0 12.2 %shard_map.82 = (bf16[2,2,512,128]{3,2,1,0:T(8,128)(2,1)}, s32[8]{0:T(128)}) custom-call(bf16[128,128,128]{2,1,0:T(8,128)(2,1)} %bitcast.9, bf16[4,256,2048]{2,1,0:T(8,128)(2,1)} %constant.8.clone.high_ref, bf16[4,256,2048]{2,1,0:T(8,128)(2,1)} %constant.9.clone.low_ref, bf16[512,512]{1,0:T(8,128)(2,1)} %constant.10.clone.near_ref, s32[8,7]{1,0:T(8,128)} %offsets_ref.1, ...), custom_call_target="tpu_custom_call" | custom-call | tf_op jit(solution)/shard_map/pallas_call | solution.py:187
  12.2 0.0 copy-start
  12.2 0.0 copy-start.1
  12.2 73.5 %shard_map.83 = bf16[8,4,2048,128]{3,2,1,0:T(8,128)(2,1)} custom-call(bf16[2048,128]{1,0:T(8,128)(2,1)} %bitcast.10), custom_call_target="tpu_custom_call" | custom-call | tf_op jit(solution)/shard_map/pallas_call | solution.py:355
  85.8 0.0 copy-done
  85.8 0.0 copy-done.1
  85.8 20.7 %shard_map.84 = f32[32,2,128,256]{3,2,1,0:T(8,128)} custom-call(s32[8]{0:T(128)S(1)} %copy-done.1, bf16[8,4,2,2,512,128]{5,4,3,2,1,0:T(8,128)(2,1)} %bitcast.7, bf16[8,4,2,2,512,128]{5,4,3,2,1,0:T(8,128)(2,1)} %bitcast.8, bf16[256,1024]{1,0:T(8,128)(2,1)S(1)} %copy-done), custom_call_target="tpu_custom_call" | custom-call | tf_op jit(solution)/shard_map/pallas_call | solution.py:436
Async XLA Ops:
  12.2 73.6 %copy-start = (bf16[256,1024]{1,0:T(8,128)(2,1)S(1)}, bf16[256,1024]{1,0:T(8,128)(2,1)}, u32[]{:S(2)}) copy-start(bf16[256,1024]{1,0:T(8,128)(2,1)} %constant.11.clone.table_ref) | copy-start | bytes 1572868
  12.2 73.6 %copy-start.1 = (s32[8]{0:T(128)S(1)}, s32[8]{0:T(128)}, u32[]{:S(2)}) copy-start(s32[8]{0:T(128)} %get-tuple-element.7.index_ref) | copy-start | bytes 100

commit v7 on v6

--- a/solution.py
+++ b/solution.py
@@ -205,6 +205,8 @@
 PLANES = 4
 MESH = pl.DeviceIdType.MESH
 LINE_ROWS = 1664
+Z_AT = 17
+ON_AT = 13
 
 
 def gather_kernel(own_ref, all_ref, z_send, z_recv, p_send, p_recv, c_send, c_recv,
@@ -303,6 +305,11 @@
             for half in (0, 1):
                 to_twin(3, other, line_half[half], c_send, c_recv, half)
 
+        def line_arrives(other):
+            landed(all_ref.at[chan, other, line], z_recv.at[other, 0])
+            along(0, other, line, z_send, z_recv)
+            line_out(other)
+
         def rest_line(other):
             for block in range(4):
                 landed(all_ref.at[blocks[block], other, rest], bz_recv.at[other, block])
@@ -324,17 +331,17 @@
         finish(z, rest_half, bp_recv)
         along(3, z, rest, bz_send, bz_recv)
         to_twin(3, z, rest, bc_send, bc_recv, 0)
+        events = [(ON_AT, line_on, z), (ON_AT + 3, line_finish, z)]
         for k in range(1, PLANES):
-            landed(all_ref.at[chan, order[k], line], z_recv.at[order[k], 0])
-            along(0, order[k], line, z_send, z_recv)
-            line_out(order[k])
-            line_on(order[k - 1])
-            rest_line(order[k])
-            if k > 1:
-                line_finish(order[k - 2])
-        line_on(order[-1])
-        line_finish(order[-2])
-        line_finish(order[-1])
+            far = abs(order[k] - z)
+            events += [
+                (Z_AT * far - (Z_AT + 1) // 2, line_arrives, order[k]),
+                (Z_AT * far, rest_line, order[k]),
+                (ON_AT * (k + 1), line_on, order[k]),
+                (ON_AT * (k + 1) + 3, line_finish, order[k]),
+            ]
+        for _, act, other in sorted(events, key=lambda event: event[0]):
+            act(other)
         for other in range(PLANES):
             for block in range(4):
                 ref = all_ref.at[twin_blocks[block], other]
@@ -391,7 +398,7 @@
         mask = (
             lax.broadcasted_iota(jnp.int32, (rows, GROUP, depth), 2) % GROUP
             == lax.broadcasted_iota(jnp.int32, (rows, GROUP, depth), 1)
-        )
+        ).astype(jnp.bfloat16)
         for g in range(FCHUNK // GROUP):
             span = slice(g * GROUP, (g + 1) * GROUP)
             firsts, plain, turned = [], [], []
@@ -402,8 +409,8 @@
                     plain += [re, im]
                     turned += [-im, re]
             left = dot_nt(select, jnp.concatenate(firsts, axis=0))
-            wide = jnp.broadcast_to(left[:, None, :], (rows, GROUP, depth))
-            wide = jnp.where(mask, wide, 0.0).reshape(rows * GROUP, depth).astype(jnp.bfloat16)
+            wide = jnp.broadcast_to(left.astype(jnp.bfloat16)[:, None, :], (rows, GROUP, depth))
+            wide = (wide * mask).reshape(rows * GROUP, depth)
             right = jnp.concatenate(
                 [jnp.concatenate(plain, axis=0), jnp.concatenate(turned, axis=0)], axis=1
             )

time: 107 us -> 112 us (1.047)
  Pallas kernels: 106 us -> 112 us
    pallas_call x1, Pallas kernels: 73.5 us -> 78.8 us  [gather(): pl.pallas_call(gather_kernel, in_specs=[pl.BlockSpec(memory_space=pl.ANY)...]
where the time goes in v7:
time: 112 us
  Pallas kernels  112 us (100%)
    pallas_call x1, Pallas kernels, gather(): pl.pallas_call(gather_kernel, in_specs=[pl.BlockSpec(memory_space=pl.ANY)...  78.8 us
    pallas_call x1, Pallas kernels, stack(): pl.pallas_call(functools.partial(stack_kernel, norm_factor, parts, segs,...  21.1 us
    pallas_call x1, Pallas kernels, whiten(): pl.pallas_call(whiten_kernel, grid=(4,), in_specs=[once(laid.shape), tabl...  12.2 us

profile of v7, /device:TPU:1, one launch (start us, length us, event | category | flops | bytes accessed | tf_op | source)
XLA Modules:
  0.0 112.1 jit_solution(17314958636451625189)
XLA Ops:
  0.0 12.2 %shard_map.82 = (bf16[2,2,512,128]{3,2,1,0:T(8,128)(2,1)}, s32[8]{0:T(128)}) custom-call(bf16[128,128,128]{2,1,0:T(8,128)(2,1)} %bitcast.9, bf16[4,256,2048]{2,1,0:T(8,128)(2,1)} %constant.8.clone.high_ref, bf16[4,256,2048]{2,1,0:T(8,128)(2,1)} %constant.9.clone.low_ref, bf16[512,512]{1,0:T(8,128)(2,1)} %constant.10.clone.near_ref, s32[8,7]{1,0:T(8,128)} %offsets_ref.1, ...), custom_call_target="tpu_custom_call" | custom-call | tf_op jit(solution)/shard_map/pallas_call | solution.py:187
  12.2 0.0 copy-start
  12.2 0.0 copy-start.1
  12.2 78.8 %shard_map.83 = bf16[8,4,2048,128]{3,2,1,0:T(8,128)(2,1)} custom-call(bf16[2048,128]{1,0:T(8,128)(2,1)} %bitcast.10), custom_call_target="tpu_custom_call" | custom-call | tf_op jit(solution)/shard_map/pallas_call | solution.py:362
  91.0 0.0 copy-done
  91.0 0.0 copy-done.1
  91.0 21.1 %shard_map.84 = f32[32,2,128,256]{3,2,1,0:T(8,128)} custom-call(s32[8]{0:T(128)S(1)} %copy-done.1, bf16[8,4,2,2,512,128]{5,4,3,2,1,0:T(8,128)(2,1)} %bitcast.7, bf16[8,4,2,2,512,128]{5,4,3,2,1,0:T(8,128)(2,1)} %bitcast.8, bf16[256,1024]{1,0:T(8,128)(2,1)S(1)} %copy-done), custom_call_target="tpu_custom_call" | custom-call | tf_op jit(solution)/shard_map/pallas_call | solution.py:443
Async XLA Ops:
  12.2 78.8 %copy-start = (bf16[256,1024]{1,0:T(8,128)(2,1)S(1)}, bf16[256,1024]{1,0:T(8,128)(2,1)}, u32[]{:S(2)}) copy-start(bf16[256,1024]{1,0:T(8,128)(2,1)} %constant.11.clone.table_ref) | copy-start | bytes 1572868
  12.2 78.8 %copy-start.1 = (s32[8]{0:T(128)S(1)}, s32[8]{0:T(128)}, u32[]{:S(2)}) copy-start(s32[8]{0:T(128)} %get-tuple-element.7.index_ref) | copy-start | bytes 100

commit v8 on v6

--- a/solution.py
+++ b/solution.py
@@ -311,7 +311,6 @@
 
         along(0, z, line, z_send, z_recv)
         outward(z, rest_half, bp_send, bp_recv)
-        along(0, z, rest, bz_send, bz_recv)
         to_twin(0, z, rest, bc_send, bc_recv, 0)
         local = pltpu.make_async_copy(own_ref, all_ref.at[chan, z], own_sem)
         local.start()
@@ -319,22 +318,26 @@
         for first in (0, 1):
             onward(z, rest_half, bp_send, bp_recv, first)
         for block in (1, 2):
-            along(block, z, rest, bz_send, bz_recv)
             to_twin(block, z, rest, bc_send, bc_recv, 0)
-        finish(z, rest_half, bp_recv)
-        along(3, z, rest, bz_send, bz_recv)
-        to_twin(3, z, rest, bc_send, bc_recv, 0)
         for k in range(1, PLANES):
             landed(all_ref.at[chan, order[k], line], z_recv.at[order[k], 0])
             along(0, order[k], line, z_send, z_recv)
             line_out(order[k])
+            if k == 1:
+                finish(z, rest_half, bp_recv)
+                to_twin(3, z, rest, bc_send, bc_recv, 0)
+            if k == PLANES - 1:
+                for block in range(4):
+                    along(block, z, rest, bz_send, bz_recv)
             line_on(order[k - 1])
-            rest_line(order[k])
             if k > 1:
                 line_finish(order[k - 2])
+        rest_line(order[1])
+        rest_line(order[2])
         line_on(order[-1])
         line_finish(order[-2])
         line_finish(order[-1])
+        rest_line(order[3])
         for other in range(PLANES):
             for block in range(4):
                 ref = all_ref.at[twin_blocks[block], other]

time: 107 us -> 110 us (1.028)
  Pallas kernels: 106 us -> 110 us
    pallas_call x1, Pallas kernels: 73.5 us -> 77 us  [gather(): pl.pallas_call(gather_kernel, in_specs=[pl.BlockSpec(memory_space=pl.ANY)...]
where the time goes in v8:
time: 110 us
  Pallas kernels  110 us (100%)
    pallas_call x1, Pallas kernels, gather(): pl.pallas_call(gather_kernel, in_specs=[pl.BlockSpec(memory_space=pl.ANY)...  77 us
    pallas_call x1, Pallas kernels, stack(): pl.pallas_call(functools.partial(stack_kernel, norm_factor, parts, segs,...  20.7 us
    pallas_call x1, Pallas kernels, whiten(): pl.pallas_call(whiten_kernel, grid=(4,), in_specs=[once(laid.shape), tabl...  12.2 us

profile of v8, /device:TPU:1, one launch (start us, length us, event | category | flops | bytes accessed | tf_op | source)
XLA Modules:
  0.0 109.9 jit_solution(14107395840176373657)
XLA Ops:
  0.0 12.2 %shard_map.82 = (bf16[2,2,512,128]{3,2,1,0:T(8,128)(2,1)}, s32[8]{0:T(128)}) custom-call(bf16[128,128,128]{2,1,0:T(8,128)(2,1)} %bitcast.9, bf16[4,256,2048]{2,1,0:T(8,128)(2,1)} %constant.8.clone.high_ref, bf16[4,256,2048]{2,1,0:T(8,128)(2,1)} %constant.9.clone.low_ref, bf16[512,512]{1,0:T(8,128)(2,1)} %constant.10.clone.near_ref, s32[8,7]{1,0:T(8,128)} %offsets_ref.1, ...), custom_call_target="tpu_custom_call" | custom-call | tf_op jit(solution)/shard_map/pallas_call | solution.py:187
  12.2 0.0 copy-start
  12.2 0.0 copy-start.1
  12.2 77.0 %shard_map.83 = bf16[8,4,2048,128]{3,2,1,0:T(8,128)(2,1)} custom-call(bf16[2048,128]{1,0:T(8,128)(2,1)} %bitcast.10), custom_call_target="tpu_custom_call" | custom-call | tf_op jit(solution)/shard_map/pallas_call | solution.py:358
  89.2 0.0 copy-done
  89.2 0.0 copy-done.1
  89.3 20.7 %shard_map.84 = f32[32,2,128,256]{3,2,1,0:T(8,128)} custom-call(s32[8]{0:T(128)S(1)} %copy-done.1, bf16[8,4,2,2,512,128]{5,4,3,2,1,0:T(8,128)(2,1)} %bitcast.7, bf16[8,4,2,2,512,128]{5,4,3,2,1,0:T(8,128)(2,1)} %bitcast.8, bf16[256,1024]{1,0:T(8,128)(2,1)S(1)} %copy-done), custom_call_target="tpu_custom_call" | custom-call | tf_op jit(solution)/shard_map/pallas_call | solution.py:439
Async XLA Ops:
  12.2 77.1 %copy-start = (bf16[256,1024]{1,0:T(8,128)(2,1)S(1)}, bf16[256,1024]{1,0:T(8,128)(2,1)}, u32[]{:S(2)}) copy-start(bf16[256,1024]{1,0:T(8,128)(2,1)} %constant.11.clone.table_ref) | copy-start | bytes 1572868
  12.2 77.1 %copy-start.1 = (s32[8]{0:T(128)S(1)}, s32[8]{0:T(128)}, u32[]{:S(2)}) copy-start(s32[8]{0:T(128)} %get-tuple-element.7.index_ref) | copy-start | bytes 100

commit v9 on v6

--- a/solution.py
+++ b/solution.py
@@ -204,7 +204,7 @@
 
 PLANES = 4
 MESH = pl.DeviceIdType.MESH
-LINE_ROWS = 1664
+LINE_ROWS = 1792
 
 
 def gather_kernel(own_ref, all_ref, z_send, z_recv, p_send, p_recv, c_send, c_recv,

time: 107 us -> 105 us (0.981)
    pallas_call x1, Pallas kernels: 73.5 us -> 72.2 us  [gather(): pl.pallas_call(gather_kernel, in_specs=[pl.BlockSpec(memory_space=pl.ANY)...]
where the time goes in v9:
time: 105 us
  Pallas kernels  105 us (100%)
    pallas_call x1, Pallas kernels, gather(): pl.pallas_call(gather_kernel, in_specs=[pl.BlockSpec(memory_space=pl.ANY)...  72.2 us
    pallas_call x1, Pallas kernels, stack(): pl.pallas_call(functools.partial(stack_kernel, norm_factor, parts, segs,...  20.7 us
    pallas_call x1, Pallas kernels, whiten(): pl.pallas_call(whiten_kernel, grid=(4,), in_specs=[once(laid.shape), tabl...  12.2 us

profile of v9, /device:TPU:1, one launch (start us, length us, event | category | flops | bytes accessed | tf_op | source)
XLA Modules:
  0.0 105.1 jit_solution(2934961252408795612)
XLA Ops:
  0.0 12.2 %shard_map.82 = (bf16[2,2,512,128]{3,2,1,0:T(8,128)(2,1)}, s32[8]{0:T(128)}) custom-call(bf16[128,128,128]{2,1,0:T(8,128)(2,1)} %bitcast.9, bf16[4,256,2048]{2,1,0:T(8,128)(2,1)} %constant.8.clone.high_ref, bf16[4,256,2048]{2,1,0:T(8,128)(2,1)} %constant.9.clone.low_ref, bf16[512,512]{1,0:T(8,128)(2,1)} %constant.10.clone.near_ref, s32[8,7]{1,0:T(8,128)} %offsets_ref.1, ...), custom_call_target="tpu_custom_call" | custom-call | tf_op jit(solution)/shard_map/pallas_call | solution.py:187
  12.2 0.0 copy-start
  12.2 0.0 copy-start.1
  12.2 72.2 %shard_map.83 = bf16[8,4,2048,128]{3,2,1,0:T(8,128)(2,1)} custom-call(bf16[2048,128]{1,0:T(8,128)(2,1)} %bitcast.10), custom_call_target="tpu_custom_call" | custom-call | tf_op jit(solution)/shard_map/pallas_call | solution.py:355
  84.4 0.0 copy-done
  84.4 0.0 copy-done.1
  84.4 20.7 %shard_map.84 = f32[32,2,128,256]{3,2,1,0:T(8,128)} custom-call(s32[8]{0:T(128)S(1)} %copy-done.1, bf16[8,4,2,2,512,128]{5,4,3,2,1,0:T(8,128)(2,1)} %bitcast.7, bf16[8,4,2,2,512,128]{5,4,3,2,1,0:T(8,128)(2,1)} %bitcast.8, bf16[256,1024]{1,0:T(8,128)(2,1)S(1)} %copy-done), custom_call_target="tpu_custom_call" | custom-call | tf_op jit(solution)/shard_map/pallas_call | solution.py:436
Async XLA Ops:
  12.2 72.2 %copy-start = (bf16[256,1024]{1,0:T(8,128)(2,1)S(1)}, bf16[256,1024]{1,0:T(8,128)(2,1)}, u32[]{:S(2)}) copy-start(bf16[256,1024]{1,0:T(8,128)(2,1)} %constant.11.clone.table_ref) | copy-start | bytes 1572868
  12.2 72.2 %copy-start.1 = (s32[8]{0:T(128)S(1)}, s32[8]{0:T(128)}, u32[]{:S(2)}) copy-start(s32[8]{0:T(128)} %get-tuple-element.7.index_ref) | copy-start | bytes 100
